TPU v7x, 32 devices: a whole 2x2x4 slice. The times are simulated.
32 devices in a mesh: cfg: 2 (over core), tok: 16 (over z, y, x).
Axes of the slice: x: 2, y: 2, z: 4, core: 2. Of those that a mesh axis runs over, the one named last changes fastest.
Arguments:
- hidden_in: bfloat16 [3072, 1152], P('tok'), may hold values from -6 to 6
- noisy_latent: float32 [3072, 16], P('tok'), may hold values from -6 to 6
- piece_rows: int32 [2, 8], replicated, may hold values from 1 to 192, 1024 in all within a row
- modulation: float32 [2, 2, 8, 1152], P('cfg'), may hold values from -3 to 3
- qkv_weight: bfloat16 [16, 1152, 432], P('tok'), may hold values from -1 to 1, as said below
- proj_weight: bfloat16 [16, 1152, 144], P('tok'), may hold values from -1 to 1, as said below
- up_weight: bfloat16 [16, 1152, 576], P('tok'), may hold values from -1 to 1, as said below
- down_weight: bfloat16 [16, 1152, 576], P('tok'), may hold values from -1 to 1, as said below
- final_weight: bfloat16 [1152, 16], replicated, may hold values from -0.1875 to 0.1875
- guidance: float32 [2], replicated, may hold values from 1.5 to 4.5
- solver_coef: float32 [2, 2], replicated, may hold values from 0.3 to 1.2
Outputs:
- next_latent: float32 [3072, 16], P('tok')
- block_out: bfloat16 [2, 3072, 1152], P('cfg', 'tok')
Inputs may be any that keep to these rules, and one draw needn't show every extreme that they name: Row l of piece_rows sums to 1024; in every row the largest entry is 192. `qkv_weight`: copy i equals copy i % 8. `proj_weight`: copy i equals copy i % 8. `up_weight`: copy i equals copy i % 8. `down_weight`: copy i equals copy i % 8.
All inputs are finite; a program needn't handle non-finite values.
Results may differ from a plain program's by a relative error of at most 0.008.
Values may be sent and summed in bfloat16 or wider, within the bound.
No kernel may reach another device: no remote copies, remote signals or barrier semaphores. Data moves between devices by JAX's collectives and lax.ppermute only.
A program may use at most 64 MiB of HBM per device.

v0:
```python
import functools
import math

import jax
import jax.numpy as jnp
from jax import lax
from jax.experimental import pallas as pl
from jax.experimental.pallas import tpu as pltpu
from jax.sharding import PartitionSpec as P

HEAD_DIM = 72
GROUP = 8
LEN = 1024
LANES = 128
ALIGN = 16
LARGE = ((1, 2, 4), (2, 4, 1))
SMALL = (4, 1, 2)
PROJ = ((2, 4, 1), (4, 1, 2))
HEADS_TO = ((2, 4, 1), (4, 1, 2))
FAR_EARLY = (80, 320)
CHUNKS = 3
F32 = jnp.float32
BF16 = jnp.bfloat16


def permute_by(block, offsets):
    count = lax.axis_size("tok")
    route = [
        (half * count + i, half * count + (i ^ offset))
        for half, offset in enumerate(offsets)
        for i in range(count)
    ]
    return lax.ppermute(block, ("cfg", "tok"), route)


def from_other_half(block):
    return lax.ppermute(block, "cfg", [(0, 1), (1, 0)])


def after(value, *earlier):
    return lax.optimization_barrier((value,) + earlier)[0]


def place():
    pos = lax.axis_index("tok")
    return lax.axis_index("cfg"), pos // GROUP, pos % GROUP


def normalized(values):
    center = values - jnp.mean(values, axis=-1, keepdims=True)
    spread = jnp.mean(center * center, axis=-1, keepdims=True)
    return center * lax.rsqrt(spread + 1e-06)


def mod_row(mod_ref, latent, k):
    return mod_ref[latent, k : k + 1, :]


def call(kernel, out_shape, operands, scratch=(), specs=None, flops=0, name=None, vmem=40):
    whole = pl.BlockSpec(memory_space=pltpu.VMEM)
    moved = sum(math.prod(o.shape) * o.dtype.itemsize for o in operands)
    return pl.pallas_call(
        kernel,
        out_shape=out_shape,
        in_specs=specs or [whole] * len(operands),
        out_specs=jax.tree.map(lambda _: whole, out_shape),
        scratch_shapes=list(scratch),
        compiler_params=pltpu.CompilerParams(vmem_limit_bytes=vmem << 20),
        cost_estimate=pl.CostEstimate(flops=flops, bytes_accessed=moved, transcendentals=0),
        name=name,
    )(*operands)


def first_kernel(hidden_ref, up_ref, down_ref, large_ref, small_ref, sems):
    core, _, _ = place()
    half = hidden_ref.shape[0] // 2
    large, small = large_ref.shape[0], half - large_ref.shape[0]
    first = pl.multiple_of(core * half, 32)
    copies = [
        pltpu.make_async_copy(hidden_ref.at[pl.ds(first, large)], large_ref, sems.at[0]),
        pltpu.make_async_copy(
            hidden_ref.at[pl.ds(first + large, small)], small_ref.at[pl.ds(0, small)], sems.at[1]
        ),
    ]
    for copy in copies:
        copy.start()
    rest = small_ref.shape[0] - small

    def bring(weight_ref):
        copy = pltpu.make_async_copy(
            weight_ref.at[pl.ds(0, rest)], small_ref.at[pl.ds(small, rest)], sems.at[2]
        )
        copy.start()
        copy.wait()

    pl.when(core == 0)(lambda: bring(up_ref))
    pl.when(core == 1)(lambda: bring(down_ref))
    for copy in copies:
        copy.wait()


def first_payloads(hidden_in, up, down, large, small, weight_rows):
    width = hidden_in.shape[1]
    return call(
        first_kernel,
        (
            jax.ShapeDtypeStruct((large, width), BF16),
            jax.ShapeDtypeStruct((small + weight_rows, width), BF16),
        ),
        (hidden_in, up, down),
        scratch=[pltpu.SemaphoreType.DMA((3,))],
        specs=[pl.BlockSpec(memory_space=pl.ANY)] * 3,
        name="first",
        vmem=63,
    )


def pad_weight(weight_ref, padded):
    weight = weight_ref[...].astype(F32)
    unused = jnp.zeros((LANES - HEAD_DIM, weight.shape[1]), F32)
    for part in range(weight.shape[0] // HEAD_DIM):
        rows = jnp.concatenate([weight[part * HEAD_DIM : (part + 1) * HEAD_DIM], unused])
        padded[part * LANES : (part + 1) * LANES, :] = rows.astype(BF16)


def qkv_kernel(row_counts, mod_ref, weight_ref, *refs):
    row_refs, (out_ref, *made, normed) = refs[: len(row_counts)], refs[len(row_counts) :]
    _, latent, _ = place()
    shift, scale = mod_row(mod_ref, latent, 0), 1.0 + mod_row(mod_ref, latent, 1)
    chunk = 32
    at = 0
    for ref, count in zip(row_refs, row_counts):
        for low in range(0, count, chunk):
            rows = ref[low : low + chunk, :].astype(F32)
            normed[at : at + chunk, :] = (normalized(rows) * scale + shift).astype(BF16)
            at += chunk
    padded = weight_ref
    if made:
        padded = made[0]
        pad_weight(weight_ref, padded)
    lane = lax.broadcasted_iota(jnp.int32, (1, padded.shape[0]), 1)
    width = padded.shape[0] // 3
    factor = jnp.where(lane < width, HEAD_DIM ** (-0.5) * math.log2(math.e), 1.0)
    ones = jnp.where((lane >= 2 * width) & (lane % LANES == HEAD_DIM), 1.0, 0.0)
    block = at // 2
    for low in range(0, at, block):
        out = lax.dot_general(
            normed[low : low + block, :], padded[...], (((1,), (1,)), ((), ())), preferred_element_type=F32
        )
        out_ref[low : low + block, :] = (out * factor + ones).astype(BF16)


def qkv_rows(modulation, weight, pieces, row_counts, make_padded, name):
    count, width = sum(row_counts), weight.shape[1]
    padded_rows = weight.shape[0] // HEAD_DIM * LANES if make_padded else weight.shape[0]
    outs = [jax.ShapeDtypeStruct((count, padded_rows), BF16)]
    if make_padded:
        outs.append(jax.ShapeDtypeStruct((padded_rows, width), BF16))
    return call(
        functools.partial(qkv_kernel, row_counts),
        tuple(outs),
        (modulation, weight) + tuple(pieces),
        scratch=[pltpu.VMEM((count, width), BF16)],
        flops=2 * count * width * padded_rows,
        name=name,
    )


def position(order, offset):
    return sum(1 << i for i, bit in enumerate(order) if offset & bit)


def spread(order, index):
    return sum(bit for i, bit in enumerate(order) if index >> i & 1)


def attention_kernel(cap, packed_rows, counts_ref, early_ref, *refs):
    late_refs, (near_ref, far_ref, packed, out) = refs[:2], refs[2:]
    core, latent, member = place()
    half = cap // 2
    large, small = 2 * half // 3, half // 3
    width = early_ref.shape[1] // 3
    heads = width // LANES
    counts = [counts_ref[latent, member ^ d] for d in range(GROUP)]
    starts = [jnp.int32(0)]
    for d in range(GROUP):
        starts.append(starts[-1] + (counts[d] + ALIGN - 1) // ALIGN * ALIGN)
    total_rows = packed.shape[0]
    spare = total_rows - LEN
    packed[LEN:, :] = jnp.zeros((spare, packed.shape[1]), BF16)
    def lay(own_core):
        for d in range(GROUP):
            for k in range(2):
                away = own_core != k
                for is_small in range(2):
                    size = small if is_small else large
                    first = k * half + is_small * large
                    where = position(SMALL if is_small else LARGE[k], d)
                    source = early_ref
                    if where == 0:
                        base = first
                    elif where < 4:
                        base = cap + is_small * 3 * large + (where - 1) * size + away * 3 * half
                    else:
                        source = late_refs[away]
                        base = is_small * 4 * large + (where - 4) * size
                    packed[pl.ds(pl.multiple_of(starts[d] + first, ALIGN), size), :] = source[
                        base : base + size, :
                    ]

    pl.when(core == 0)(lambda: lay(0))
    pl.when(core == 1)(lambda: lay(1))
    slot = lax.broadcasted_iota(jnp.int32, (1, packed_rows), 1)
    valid = jnp.zeros((1, packed_rows), jnp.bool_)
    for d in range(GROUP):
        valid = valid | ((slot >= starts[d]) & (slot < starts[d] + counts[d]))
    bias = jnp.where(valid, 0.0, -1e30)
    out[LEN:, :] = jnp.zeros((spare, out.shape[1]), F32)
    block = packed_rows // 3
    for low in range(0, packed_rows, block):
        for head in range(heads):
            lanes = head * LANES
            queries = packed[low : low + block, lanes : lanes + LANES]
            keys = packed[:packed_rows, width + lanes : width + lanes + LANES]
            values = packed[:packed_rows, 2 * width + lanes : 2 * width + lanes + LANES]
            scores = lax.dot_general(
                queries, keys, (((1,), (1,)), ((), ())), preferred_element_type=F32
            )
            scores = scores + bias
            peak = jnp.max(scores, axis=-1, keepdims=True)
            probs = jnp.exp2(scores - peak).astype(BF16)
            mixed = jnp.dot(probs, values, preferred_element_type=F32)
            mixed = mixed / mixed[:, HEAD_DIM : HEAD_DIM + 1]
            out[low : low + block, lanes : lanes + LANES] = mixed
    targets = [
        jnp.where(core == 0, starts[spread(HEADS_TO[0], j)], starts[spread(HEADS_TO[1], j)])
        for j in range(GROUP)
    ]
    for pair in range(0, GROUP, 2):
        columns = []
        for head in range(heads):
            rows = [
                out[pl.ds(pl.multiple_of(targets[j], ALIGN), cap), head * LANES : (head + 1) * LANES]
                for j in (pair, pair + 1)
            ]
            columns.append(jnp.concatenate(rows).T[:HEAD_DIM])
        dest = near_ref if pair < GROUP // 2 else far_ref
        at = pair % (GROUP // 2) * cap
        dest[:, at : at + 2 * cap] = jnp.concatenate(columns).astype(BF16)


def attention(piece_rows, early, late, cap):
    packed_rows = LEN + GROUP * ALIGN
    total = -(-(packed_rows + cap) // 32) * 32
    width = early.shape[1] // 3
    heads = width // LANES
    shape = jax.ShapeDtypeStruct((heads * HEAD_DIM, GROUP // 2 * cap), BF16)
    return call(
        functools.partial(attention_kernel, cap, packed_rows),
        (shape, shape),
        (piece_rows, early) + tuple(late),
        scratch=[pltpu.VMEM((total, 3 * width), BF16), pltpu.VMEM((total, width), F32)],
        specs=[pl.BlockSpec(memory_space=pltpu.SMEM)] + [pl.BlockSpec(memory_space=pltpu.VMEM)] * 3,
        flops=4 * heads * packed_rows * packed_rows * LANES,
        name="attend",
    )


def project_kernel(cap, mod_ref, hidden_ref, mine_ref, mate_ref, *refs):
    proj_refs, plane_refs = refs[:8], refs[8 : 8 + GROUP // 2 - 1]
    mid_ref, mlp_ref, flat, weights = refs[8 + GROUP // 2 - 1 :]
    core, latent, member = place()
    heads = mine_ref.shape[0] // HEAD_DIM

    def put(block, j):
        offset = jnp.where(core == 0, spread(HEADS_TO[0], j), spread(HEADS_TO[1], j))
        for head in range(heads):
            rows = block[head * HEAD_DIM : (head + 1) * HEAD_DIM]
            flat[head * GROUP + offset] = rows

    put(mine_ref[...][:, :cap].astype(F32), 0)
    put(mate_ref[...][:, :cap].astype(F32), GROUP // 2)
    for j, ref in enumerate(plane_refs):
        both = ref[...].astype(F32)
        put(both[:, :cap], j + 1)
        put(both[:, cap:], (j + 1) ^ (GROUP // 2))
    for away in range(2):
        head = core if away == 0 else 1 - core
        at = 0
        for blocks, ref in zip((1, 1, 2, 4), proj_refs[4 * away : 4 * away + 4]):
            block = ref[ref.shape[0] - blocks * HEAD_DIM :, :].astype(F32)
            for row in range(0, block.shape[0], HEAD_DIM):
                offset = jnp.where(head == 0, spread(PROJ[0], at), spread(PROJ[1], at))
                weights[head * GROUP + offset] = block[row : row + HEAD_DIM]
                at += 1
    stacked = flat[...].reshape(heads * GROUP * HEAD_DIM, cap).astype(BF16)
    proj = weights[...].reshape(heads * GROUP * HEAD_DIM, weights.shape[2]).astype(BF16)
    attn_out = lax.dot_general(stacked, proj, (((0,), (0,)), ((), ())), preferred_element_type=F32)
    mid = hidden_ref[...].astype(F32) + mod_row(mod_ref, latent, 2) * attn_out
    mid_ref[...] = mid
    scale, shift = 1.0 + mod_row(mod_ref, latent, 4), mod_row(mod_ref, latent, 3)
    mlp_ref[...] = (normalized(mid) * scale + shift).astype(BF16)


def project(modulation, hidden_in, proj_parts, mine, mate, plane):
    cap, width = hidden_in.shape
    heads = mine.shape[0] // HEAD_DIM
    return call(
        functools.partial(project_kernel, cap),
        (jax.ShapeDtypeStruct((cap, width), F32), jax.ShapeDtypeStruct((cap, width), BF16)),
        (modulation, hidden_in, mine, mate) + tuple(proj_parts) + tuple(plane),
        scratch=[
            pltpu.VMEM((heads * GROUP, HEAD_DIM, cap), F32),
            pltpu.VMEM((heads * GROUP, HEAD_DIM, width), F32),
        ],
        flops=2 * cap * width * width,
        name="project",
    )


def pack_kernel(row_counts, up_ref, down_ref, *refs):
    far_refs, (up_all, down_all, sems) = refs[:-3], refs[-3:]
    core, _, _ = place()
    hidden, parts = up_ref.shape[0], len(far_refs) // 2
    own = [
        pltpu.make_async_copy(up_ref, up_all.at[pl.ds(0, hidden)], sems.at[2 * parts]),
        pltpu.make_async_copy(down_ref, down_all.at[pl.ds(0, hidden)], sems.at[2 * parts + 1]),
    ]
    for copy in own:
        copy.start()

    def fetch(dests):
        copies = []
        for d, dest in enumerate(dests):
            at = hidden
            for rows, ref in zip(row_counts, far_refs[parts * d : parts * (d + 1)]):
                source = ref.at[pl.ds(ref.shape[0] - rows, rows)]
                copies.append(
                    pltpu.make_async_copy(source, dest.at[pl.ds(at, rows)], sems.at[len(copies)])
                )
                at += rows
        for copy in copies:
            copy.start()
        for copy in copies:
            copy.wait()

    pl.when(core == 0)(lambda: fetch((up_all, down_all)))
    pl.when(core == 1)(lambda: fetch((down_all, up_all)))
    for copy in own:
        copy.wait()


def pack(up, down, far, row_counts):
    hidden, width = up.shape
    both = jax.ShapeDtypeStruct((2 * hidden, width), BF16)
    return call(
        functools.partial(pack_kernel, row_counts),
        (both, both),
        (up, down) + tuple(far),
        scratch=[pltpu.SemaphoreType.DMA((2 + len(far),))],
        specs=[pl.BlockSpec(memory_space=pl.ANY)] * (2 + len(far)),
        name="pack",
    )


def mlp_kernel(row_count, out_count, up_ref, down_ref, *refs):
    row_refs, out_refs, rows = refs[:row_count], refs[row_count:-1], refs[-1]
    at = 0
    for ref in row_refs:
        rows[at : at + ref.shape[0], :] = ref[...]
        at += ref.shape[0]
    units = lax.dot_general(
        rows[...], up_ref[...], (((1,), (1,)), ((), ())), preferred_element_type=F32
    )
    units = 0.5 * units * (1.0 + jnp.tanh(0.7978845608 * (units + 0.044715 * (units * units * units))))
    partial = jnp.dot(units.astype(BF16), down_ref[...], preferred_element_type=F32)
    at = 0
    for ref in out_refs:
        ref[...] = partial[at : at + ref.shape[0]].astype(ref.dtype)
        at += ref.shape[0]


def mlp_rows(pieces, packed, out_rows, dtype, name):
    count = sum(p.shape[0] for p in pieces)
    hidden, width = packed[0].shape
    outs = tuple(jax.ShapeDtypeStruct((rows, width), dtype) for rows in out_rows)
    return call(
        functools.partial(mlp_kernel, len(pieces), len(outs)),
        outs,
        tuple(packed) + tuple(pieces),
        scratch=[pltpu.VMEM((count, width), BF16)],
        flops=4 * count * width * hidden,
        name=name,
    )


def final_kernel(
    counts_ref, guide_ref, coef_ref, mod_ref, mid_ref, part_ref, noisy_ref, weight_ref,
    *refs,
):
    core, latent, member = place()
    cap = mid_ref.shape[0]
    sum_refs, (block_ref, pred_ref, base_ref, total) = refs[:-4], refs[-4:]
    chunk = cap // CHUNKS
    for i, (first, second) in enumerate(zip(sum_refs[:CHUNKS], sum_refs[CHUNKS:])):
        rows = slice(i * chunk, (i + 1) * chunk)
        total[rows, :] = part_ref[rows, :] + first[:chunk, :].astype(F32) + second[...].astype(F32)
    rows = (mid_ref[...] + mod_row(mod_ref, latent, 5) * total[...]).astype(BF16).astype(F32)
    count = counts_ref[latent, member]
    rows = jnp.where(lax.broadcasted_iota(jnp.int32, (cap, 1), 0) < count, rows, 0.0)
    block_ref[...] = rows.astype(BF16)
    scale, shift = 1.0 + mod_row(mod_ref, latent, 7), mod_row(mod_ref, latent, 6)
    final_in = (normalized(rows) * scale + shift).astype(BF16)
    pred = lax.dot_general(
        weight_ref[...], final_in, (((1,), (1,)), ((), ())), preferred_element_type=F32
    )
    guide = guide_ref[latent]
    valid = lax.broadcasted_iota(jnp.int32, (1, cap), 1) < count
    weighted = (-coef_ref[latent, 1] * jnp.where(core == 0, guide, 1.0 - guide)) * pred
    pred_ref[...] = jnp.where(valid, weighted, 0.0)
    base_ref[...] = jnp.where(valid, coef_ref[latent, 0] * noisy_ref[...], 0.0)


def final(scalars, modulation, mid, part, noisy, weight, firsts, seconds):
    cap, width = mid.shape
    smem, vmem = pl.BlockSpec(memory_space=pltpu.SMEM), pl.BlockSpec(memory_space=pltpu.VMEM)
    flat = jax.ShapeDtypeStruct(noisy.shape, F32)
    return call(
        final_kernel,
        (jax.ShapeDtypeStruct((cap, width), BF16), flat, flat),
        tuple(scalars) + (modulation, mid, part, noisy, weight) + tuple(firsts) + tuple(seconds),
        scratch=[pltpu.VMEM((cap, width), F32)],
        specs=[smem] * 3 + [vmem] * (5 + 2 * CHUNKS),
        flops=2 * cap * width * weight.shape[0],
        name="finish",
    )


def shards(
    hidden_in,
    noisy_latent,
    piece_rows,
    modulation,
    qkv_weight,
    proj_weight,
    up_weight,
    down_weight,
    final_weight,
    guidance,
    solver_coef,
):
    cap, width = hidden_in.shape
    half = cap // 2
    large, small = 2 * half // 3, half // 3
    core, _, _ = place()
    modulation = modulation[0]
    qkv_rows_t, proj_t, up_t, down_t = (
        w[0].T for w in (qkv_weight, proj_weight, up_weight, down_weight)
    )

    hidden = up_t.shape[0]
    cuts = (0, FAR_EARLY[0], sum(FAR_EARLY), hidden)
    large_rows, small_rows = first_payloads(hidden_in, up_t, down_t, large, small, cuts[1])
    proj_rows = None
    got, away = [], []
    for step in range(3):
        payload = large_rows if step == 0 else jnp.concatenate([large_rows, proj_rows])
        got_large = permute_by(payload, [order[step] for order in LARGE])
        got_small = permute_by(small_rows, [SMALL[step]] * 2)
        if step == 0:
            up_t, down_t, _ = lax.optimization_barrier((up_t, down_t, got_large))
            sent = [
                jnp.where(core == 0, up_t[low:high], down_t[low:high])
                for low, high in zip(cuts[1:-1], cuts[2:])
            ]
            proj_own = [
                lax.dynamic_slice_in_dim(proj_t, head * HEAD_DIM, HEAD_DIM) for head in (core, 1 - core)
            ]
            proj_rows = proj_own[0]
        elif step == 1:
            proj_rows = jnp.concatenate([proj_rows, got_large[2 * large :]])
        else:
            early, qkv_padded = qkv_rows(
                modulation,
                qkv_rows_t,
                (hidden_in, got[0][0], got[1][0], got[0][1], got[1][1])
                + (away[0][0], away[1][0], away[0][1], away[1][1]),
                (cap, large, 2 * large, small, 2 * small) + (large, 2 * large, small, 2 * small),
                True,
                "qkv_early",
            )
            got_large, got_small, early, *sent = lax.optimization_barrier(
                (got_large, got_small, early, *sent)
            )
            proj_rows = jnp.concatenate([proj_rows, got_large[4 * large :]])
        if step < 2:
            large_rows = jnp.concatenate([large_rows, got_large[: large << step]])
            small_rows = jnp.concatenate([rows[: small << step] for rows in (small_rows, got_small)])
        got.append((got_large, got_small))
        away.append((from_other_half(got_large), from_other_half(got_small)))
    proj_last = permute_by(proj_rows, [order[2] for order in PROJ])
    far = [got[0][1], permute_by(sent[0], [GROUP // 2] * 2)]
    counts = (4 * large, 4 * small)
    late = list(qkv_rows(modulation, qkv_padded, got[2], counts, False, "qkv_late_own"))
    *other, late[0] = lax.optimization_barrier((*away[2], late[0]))
    late += qkv_rows(modulation, qkv_padded, other, counts, False, "qkv_late_other")
    mine, sent_heads = attention(piece_rows, early, late, cap)
    mate = permute_by(sent_heads, [order[2] for order in HEADS_TO])
    mate, proj_last = lax.optimization_barrier((mate, proj_last))
    proj_parts = [proj_own[0], got[1][0], got[2][0], proj_last]
    proj_parts += [proj_own[1], away[1][0], away[2][0], from_other_half(proj_last)]
    plane = []
    for j in range(1, GROUP // 2):
        both = jnp.concatenate([a[:, j * cap : (j + 1) * cap] for a in (mine, mate)], axis=1)
        plane.append(permute_by(both, [spread(order, j) for order in HEADS_TO]))
    far[1], *plane = lax.optimization_barrier((far[1], *plane))
    far.append(permute_by(after(sent[1], *plane), [GROUP // 2] * 2))
    mid, mlp_in = project(modulation, hidden_in, proj_parts, mine, mate, plane)

    chunk = cap // CHUNKS
    side = permute_by(mlp_in, (1, 2))
    both = [
        jnp.concatenate([rows[low : low + chunk] for rows in (mlp_in, side)])
        for low in range(0, cap, chunk)
    ]
    across = [permute_by(rows, (2, 1)) for rows in both]
    far[2] = after(far[2], *both)
    far += [away[0][1]] + [from_other_half(rows) for rows in far[1:]]
    packed = pack(up_t, down_t, far, [high - low for low, high in zip(cuts[:-1], cuts[1:])])
    sums = [
        mlp_rows((rows,), packed, (2 * chunk,), BF16, f"mlp_far{i}")[0] for i, rows in enumerate(across)
    ]
    firsts = [permute_by(rows, (2, 1)) for rows in sums]
    part, *side_parts = mlp_rows(
        (after(mlp_in, *sums), side), packed, (cap,) + (chunk,) * CHUNKS, F32, "mlp_near"
    )
    seconds = [
        permute_by((rows + first[chunk:].astype(F32)).astype(BF16), (1, 2))
        for rows, first in zip(side_parts, firsts)
    ]
    block_rows, pred, base = final(
        (piece_rows, guidance, solver_coef),
        modulation,
        mid,
        part,
        noisy_latent.T,
        final_weight.T,
        firsts,
        seconds,
    )
    next_latent = base + (pred + from_other_half(pred))
    return (next_latent.T, block_rows[None])


def solution(mesh):
    placed = (
        P("tok", None),
        P("tok", None),
        P(),
        P("cfg", None, None, None),
        P("tok", None, None),
        P("tok", None, None),
        P("tok", None, None),
        P("tok", None, None),
        P(),
        P(),
        P(),
    )
    return jax.shard_map(
        shards,
        mesh=mesh,
        in_specs=placed,
        out_specs=(P("tok", None), P("cfg", "tok", None)),
        check_vma=False,
    )
```

profile of v0, /device:TPU:0, one launch (start us, length us, event | category | flops | bytes accessed | tf_op | source)
XLA Modules:
  0.0 106.6 jit_solution(13696894226993340667)
XLA Ops:
  0.6 1.9 %first.1 = (bf16[64,1152]{1,0:T(8,128)(2,1)}, bf16[112,1152]{1,0:T(8,128)(2,1)}) custom-call(bf16[192,1152]{1,0:T(8,128)(2,1)} %hidden_ref.3, bf16[576,1152]{1,0:T(8,128)(2,1)} %bitcast.23, bf16[576,1152]{1,0:T(8,128)(2,1)} %bitcast.27), custom_call_target="tpu_custom_call" | custom-call | bytes 3096576 | tf_op jit(solution)/shard_map/first/pallas_call | solution.py:62
  2.5 3.0 %collective-permute-start = (bf16[64,1152]{1,0:T(8,128)(2,1)}, bf16[64,1152]{1,0:T(8,128)(2,1)S(1)}, u32[]{:S(2)}, u32[]{:S(2)}) collective-permute-start(bf16[64,1152]{1,0:T(8,128)(2,1)} %get-tuple-element.38), channel_id=1, source_target_pairs={{0,1},{1,0},{2,3},{3,2},{4,5},{5,4},{6,7},{7,6},{8,9},{9,8},{10,11... | collective-permute-start | bytes 442376 | tf_op jit(solution)/shard_map/ppermute | solution.py:33
  10.1 1.9 %collective-permute-start.1 = (bf16[200,1152]{1,0:T(8,128)(2,1)S(1)}, bf16[200,1152]{1,0:T(8,128)(2,1)S(1)}, u32[]{:S(2)}, u32[]{:S(2)}) collective-permute-start(bf16[200,1152]{1,0:T(8,128)(2,1)S(1)} %pad_maximum_fusion.1), channel_id=1, source_target_pairs={{0,2},{1,3},{2,0},{3,1},{4,6},{5,7},{6,4},{7,5},{8,10},{9,11},{10,... | collective-permute-start | bytes 1382408 | tf_op jit(solution)/shard_map/ppermute | solution.py:33
  12.1 2.6 %collective-permute-done.3.refs_3_.refs_0_ = bf16[112,1152]{1,0:T(8,128)(2,1)S(1)} collective-permute-done((bf16[112,1152]{1,0:T(8,128)(2,1)}, bf16[112,1152]{1,0:T(8,128)(2,1)S(1)}, u32[]{:S(2)}, u32[]{:S(2)}) %collective-permute-start.3) | collective-permute-done | bytes 258080 | tf_op jit(solution)/shard_map/ppermute | solution.py:33
  15.0 3.7 %collective-permute-done.1.refs_2_.refs_1_ = bf16[200,1152]{1,0:T(8,128)(2,1)S(1)} collective-permute-done((bf16[200,1152]{1,0:T(8,128)(2,1)S(1)}, bf16[200,1152]{1,0:T(8,128)(2,1)S(1)}, u32[]{:S(2)}, u32[]{:S(2)}) %collective-permute-start.1) | collective-permute-done | bytes 460832 | tf_op jit(solution)/shard_map/ppermute | solution.py:33
  18.8 2.0 %collective-permute-start.2 = (bf16[400,1152]{1,0:T(8,128)(2,1)S(1)}, bf16[400,1152]{1,0:T(8,128)(2,1)S(1)}, u32[]{:S(2)}, u32[]{:S(2)}) collective-permute-start(bf16[400,1152]{1,0:T(8,128)(2,1)S(1)} %get-tuple-element.75), channel_id=1, source_target_pairs={{0,4},{1,5},{2,6},{3,7},{4,0},{5,1},{6,2},{7,3},{8,12},{9,13},{10,... | collective-permute-start | bytes 2764808 | tf_op jit(solution)/shard_map/ppermute | solution.py:33
  25.1 2.5 %qkv_early.1 = (bf16[768,768]{1,0:T(8,128)(2,1)S(1)}, bf16[768,1152]{1,0:T(8,128)(2,1)S(1)}) custom-call(f32[2,8,1152]{2,1,0:T(8,128)S(1)} %bitcast.31, bf16[432,1152]{1,0:T(8,128)(2,1)S(1)} %bitcast.38, bf16[192,1152]{1,0:T(8,128)(2,1)S(1)} %copy-done.2, bf16[64,1152]{1,0:T(8,128)(2,1)S(1)} %collective-permute-done.refs_1_, ...), custom_call_target="tpu_custom_call" | custom-call | flops 1358954496 | bytes 3538944 | tf_op jit(solution)/shard_map/qkv_early/pallas_call | solution.py:62
  27.7 2.9 %collective-permute-done.5.refs_1_ = bf16[128,1152]{1,0:T(8,128)(2,1)S(1)} collective-permute-done((bf16[128,1152]{1,0:T(8,128)(2,1)S(1)}, bf16[128,1152]{1,0:T(8,128)(2,1)S(1)}, u32[]{:S(2)}, u32[]{:S(2)}) %collective-permute-start.5) | collective-permute-done | bytes 294944 | tf_op jit(solution)/shard_map/ppermute | solution.py:33
  30.6 1.7 %collective-permute-done.2.refs_0_.refs_2_ = bf16[400,1152]{1,0:T(8,128)(2,1)S(1)} collective-permute-done((bf16[400,1152]{1,0:T(8,128)(2,1)S(1)}, bf16[400,1152]{1,0:T(8,128)(2,1)S(1)}, u32[]{:S(2)}, u32[]{:S(2)}) %collective-permute-start.2) | collective-permute-done | bytes 921632 | tf_op jit(solution)/shard_map/ppermute | solution.py:33
  33.0 1.9 %collective-permute-start.13 = (bf16[288,1152]{1,0:T(8,128)(2,1)S(1)}, bf16[288,1152]{1,0:T(8,128)(2,1)S(1)}, u32[]{:S(2)}, u32[]{:S(2)}) collective-permute-start(bf16[288,1152]{1,0:T(8,128)(2,1)S(1)} %pad_maximum_fusion), channel_id=1, source_target_pairs={{0,1},{1,0},{2,3},{3,2},{4,5},{5,4},{6,7},{7,6},{8,9},{9,8},{10,11... | collective-permute-start | bytes 1990664 | tf_op jit(solution)/shard_map/ppermute | solution.py:33
  36.4 1.6 %qkv_late_own.1.refs_0_ = bf16[384,768]{1,0:T(8,128)(2,1)S(1)} custom-call(f32[2,8,1152]{2,1,0:T(8,128)S(1)} %bitcast.32, bf16[768,1152]{1,0:T(8,128)(2,1)S(1)} %get-tuple-element.46.weight_ref, bf16[400,1152]{1,0:T(8,128)(2,1)S(1)} %collective-permute-done.2.refs_0_.refs_2_, bf16[128,1152]{1,0:T(8,128)(2,1)S(1)} %collective-permute-done.5.refs_1_), custom_call_target="tpu_custom_call" | custom-call | flops 679477248 | bytes 3059712 | tf_op jit(solution)/shard_map/qkv_late_own/pallas_call | solution.py:62
  38.1 1.6 %qkv_late_other.1.refs_1_ = bf16[384,768]{1,0:T(8,128)(2,1)S(1)} custom-call(f32[2,8,1152]{2,1,0:T(8,128)S(1)} %bitcast.33, bf16[768,1152]{1,0:T(8,128)(2,1)S(1)} %get-tuple-element.46.weight_ref, bf16[400,1152]{1,0:T(8,128)(2,1)S(1)} %collective-permute-done.10.refs_0_.refs_6_, bf16[128,1152]{1,0:T(8,128)(2,1)S(1)} %collective-permute-done.11.refs_1_), custom_call_target="tpu_custom_call" | custom-call | flops 679477248 | bytes 3059712 | tf_op jit(solution)/shard_map/qkv_late_other/pallas_call | solution.py:62
  39.7 6.2 %attend.1 = (bf16[144,768]{1,0:T(8,128)(2,1)S(1)}, bf16[144,768]{1,0:T(8,128)(2,1)S(1)}) custom-call(s32[2,8]{1,0:T(2,128)S(1)} %copy-done.6, bf16[768,768]{1,0:T(8,128)(2,1)S(1)} %get-tuple-element.43.early_ref, bf16[384,768]{1,0:T(8,128)(2,1)S(1)} %qkv_late_own.1.refs_0_, bf16[384,768]{1,0:T(8,128)(2,1)S(1)} %qkv_late_other.1.refs_1_), custom_call_target="tpu_custom_call" | custom-call | flops 1358954496 | bytes 2359360 | tf_op jit(solution)/shard_map/attend/pallas_call | solution.py:62
  46.7 5.3 %collective-permute-done.12.mate_ref = bf16[144,768]{1,0:T(8,128)(2,1)S(1)} collective-permute-done((bf16[144,768]{1,0:T(8,128)(2,1)S(1)}, bf16[144,768]{1,0:T(8,128)(2,1)S(1)}, u32[]{:S(2)}, u32[]{:S(2)}) %collective-permute-start.12) | collective-permute-done | bytes 221216 | tf_op jit(solution)/shard_map/ppermute | solution.py:33
  57.0 2.4 %collective-permute-done.17.refs_9_ = bf16[144,384]{1,0:T(8,128)(2,1)S(1)} collective-permute-done((bf16[144,384]{1,0:T(8,128)(2,1)S(1)}, bf16[144,384]{1,0:T(8,128)(2,1)S(1)}, u32[]{:S(2)}, u32[]{:S(2)}) %collective-permute-start.17) | collective-permute-done | bytes 110624 | tf_op jit(solution)/shard_map/ppermute | solution.py:33
  59.4 1.7 %collective-permute-done.18.refs_10_ = bf16[144,384]{1,0:T(8,128)(2,1)S(1)} collective-permute-done((bf16[144,384]{1,0:T(8,128)(2,1)S(1)}, bf16[144,384]{1,0:T(8,128)(2,1)S(1)}, u32[]{:S(2)}, u32[]{:S(2)}) %collective-permute-start.18) | collective-permute-done | bytes 110624 | tf_op jit(solution)/shard_map/ppermute | solution.py:33
  61.9 1.9 %project.1 = (f32[192,1152]{1,0:T(8,128)S(1)}, bf16[192,1152]{1,0:T(8,128)(2,1)S(1)}) custom-call(f32[2,8,1152]{2,1,0:T(8,128)S(1)} %bitcast.34, bf16[192,1152]{1,0:T(8,128)(2,1)S(1)} %copy-done.2, bf16[144,768]{1,0:T(8,128)(2,1)S(1)} %get-tuple-element.50.mine_ref, bf16[144,768]{1,0:T(8,128)(2,1)S(1)} %collective-permute-done.12.mate_ref, ...), custom_call_target="tpu_custom_call" | custom-call | flops 509607936 | bytes 5713920 | tf_op jit(solution)/shard_map/project/pallas_call | solution.py:62
  64.5 7.7 %collective-permute-done.20.refs_1_ = bf16[192,1152]{1,0:T(8,128)(2,1)S(1)} collective-permute-done((bf16[192,1152]{1,0:T(8,128)(2,1)S(1)}, bf16[192,1152]{1,0:T(8,128)(2,1)S(1)}, u32[]{:S(2)}, u32[]{:S(2)}) %collective-permute-start.20) | collective-permute-done | bytes 442400 | tf_op jit(solution)/shard_map/ppermute | solution.py:33
  75.6 2.0 %pack.1 = (bf16[1152,1152]{1,0:T(8,128)(2,1)S(1)}, bf16[1152,1152]{1,0:T(8,128)(2,1)S(1)}) custom-call(bf16[576,1152]{1,0:T(8,128)(2,1)S(1)} %bitcast.26, bf16[576,1152]{1,0:T(8,128)(2,1)S(1)} %bitcast.30, bf16[112,1152]{1,0:T(8,128)(2,1)S(1)} %collective-permute-done.3.refs_3_.refs_0_, bf16[320,1152]{1,0:T(8,128)(2,1)S(1)} %collective-permute-done.15.refs_1_, ...), custom_call_target="tpu_custom_call" | custom-call | bytes 5455872 | tf_op jit(solution)/shard_map/pack/pallas_call | solution.py:62
  77.6 1.6 %collective-permute-done.23.refs_0_ = bf16[128,1152]{1,0:T(8,128)(2,1)S(1)} collective-permute-done((bf16[128,1152]{1,0:T(8,128)(2,1)S(1)}, bf16[128,1152]{1,0:T(8,128)(2,1)S(1)}, u32[]{:S(2)}, u32[]{:S(2)}) %collective-permute-start.23) | collective-permute-done | bytes 294944 | tf_op jit(solution)/shard_map/ppermute | solution.py:33
  88.1 2.7 %mlp_near.1 = (f32[192,1152]{1,0:T(8,128)S(1)}, f32[64,1152]{1,0:T(8,128)S(1)}, f32[64,1152]{1,0:T(8,128)S(1)}, f32[64,1152]{1,0:T(8,128)S(1)}) custom-call(bf16[1152,1152]{1,0:T(8,128)(2,1)S(1)} %get-tuple-element.64.up_ref, bf16[1152,1152]{1,0:T(8,128)(2,1)S(1)} %get-tuple-element.65.down_ref, bf16[192,1152]{1,0:T(8,128)(2,1)S(1)} %get-tuple-element.66.refs_0_, ...), custom_call_target="tpu_custom_call" | custom-call | flops 2038431744 | bytes 6193152 | tf_op jit(solution)/shard_map/mlp_near/pallas_call | solution.py:62
  93.1 4.5 %collective-permute-done.28.refs_2_ = bf16[128,1152]{1,0:T(8,128)(2,1)S(1)} collective-permute-done((bf16[128,1152]{1,0:T(8,128)(2,1)S(1)}, bf16[128,1152]{1,0:T(8,128)(2,1)S(1)}, u32[]{:S(2)}, u32[]{:S(2)}) %collective-permute-start.28) | collective-permute-done | bytes 294944 | tf_op jit(solution)/shard_map/ppermute | solution.py:33
  97.7 5.1 %collective-permute-done.31.refs_5_ = bf16[64,1152]{1,0:T(8,128)(2,1)S(1)} collective-permute-done((bf16[64,1152]{1,0:T(8,128)(2,1)S(1)}, bf16[64,1152]{1,0:T(8,128)(2,1)S(1)}, u32[]{:S(2)}, u32[]{:S(2)}) %collective-permute-start.31) | collective-permute-done | bytes 147488 | tf_op jit(solution)/shard_map/ppermute | solution.py:33
  102.8 1.9 %finish.1 = (bf16[192,1152]{1,0:T(8,128)(2,1)}, f32[16,192]{1,0:T(8,128)S(1)}, f32[16,192]{1,0:T(8,128)S(1)}) custom-call(s32[2,8]{1,0:T(2,128)S(1)} %copy-done.6, f32[2]{0:T(128)S(1)} %copy-done.8, f32[2,2]{1,0:T(2,128)S(1)} %copy-done.7, f32[2,8,1152]{2,1,0:T(8,128)S(1)} %bitcast.35, f32[192,1152]{1,0:T(8,128)S(1)} %get-tuple-element.58.mid_ref, ...), custom_call_target="tpu_custom_call" | custom-call | flops 7077888 | bytes 3219544 | tf_op jit(solution)/shard_map/finish/pallas_call | solution.py:62
  (105 shorter events, 35.1 us)
Async XLA Ops:
  2.5 6.5 %collective-permute-start = (bf16[64,1152]{1,0:T(8,128)(2,1)}, bf16[64,1152]{1,0:T(8,128)(2,1)S(1)}, u32[]{:S(2)}, u32[]{:S(2)}) collective-permute-start(bf16[64,1152]{1,0:T(8,128)(2,1)} %get-tuple-element.38), channel_id=1, source_target_pairs={{0,1},{1,0},{2,3},{3,2},{4,5},{5,4},{6,7},{7,6},{8,9},{9,8},{10,11... | collective-permute-start | bytes 442376 | tf_op jit(solution)/shard_map/ppermute | solution.py:33
  5.5 9.2 %collective-permute-start.3 = (bf16[112,1152]{1,0:T(8,128)(2,1)}, bf16[112,1152]{1,0:T(8,128)(2,1)S(1)}, u32[]{:S(2)}, u32[]{:S(2)}) collective-permute-start(bf16[112,1152]{1,0:T(8,128)(2,1)} %get-tuple-element.39), channel_id=1, source_target_pairs={{0,4},{1,5},{2,6},{3,7},{4,0},{5,1},{6,2},{7,3},{8,12},{9,13},{10,... | collective-permute-start | bytes 774152 | tf_op jit(solution)/shard_map/ppermute | solution.py:33
  10.1 8.6 %collective-permute-start.1 = (bf16[200,1152]{1,0:T(8,128)(2,1)S(1)}, bf16[200,1152]{1,0:T(8,128)(2,1)S(1)}, u32[]{:S(2)}, u32[]{:S(2)}) collective-permute-start(bf16[200,1152]{1,0:T(8,128)(2,1)S(1)} %pad_maximum_fusion.1), channel_id=1, source_target_pairs={{0,2},{1,3},{2,0},{3,1},{4,6},{5,7},{6,4},{7,5},{8,10},{9,11},{10,... | collective-permute-start | bytes 1382408 | tf_op jit(solution)/shard_map/ppermute | solution.py:33
  14.7 6.8 %collective-permute-start.4 = (bf16[64,1152]{1,0:T(8,128)(2,1)S(1)}, bf16[64,1152]{1,0:T(8,128)(2,1)S(1)}, u32[]{:S(2)}, u32[]{:S(2)}) collective-permute-start(bf16[64,1152]{1,0:T(8,128)(2,1)S(1)} %pad_maximum_fusion.6), channel_id=1, source_target_pairs={{0,1},{1,0},{2,3},{3,2},{4,5},{5,4},{6,7},{7,6},{8,9},{9,8},{10,11... | collective-permute-start | bytes 442376 | tf_op jit(solution)/shard_map/ppermute | solution.py:33
  18.8 13.5 %collective-permute-start.2 = (bf16[400,1152]{1,0:T(8,128)(2,1)S(1)}, bf16[400,1152]{1,0:T(8,128)(2,1)S(1)}, u32[]{:S(2)}, u32[]{:S(2)}) collective-permute-start(bf16[400,1152]{1,0:T(8,128)(2,1)S(1)} %get-tuple-element.75), channel_id=1, source_target_pairs={{0,4},{1,5},{2,6},{3,7},{4,0},{5,1},{6,2},{7,3},{8,12},{9,13},{10,... | collective-permute-start | bytes 2764808 | tf_op jit(solution)/shard_map/ppermute | solution.py:33
  21.5 9.1 %collective-permute-start.5 = (bf16[128,1152]{1,0:T(8,128)(2,1)S(1)}, bf16[128,1152]{1,0:T(8,128)(2,1)S(1)}, u32[]{:S(2)}, u32[]{:S(2)}) collective-permute-start(bf16[128,1152]{1,0:T(8,128)(2,1)S(1)} %pad_maximum_fusion.2), channel_id=1, source_target_pairs={{0,2},{1,3},{2,0},{3,1},{4,6},{5,7},{6,4},{7,5},{8,10},{9,11},{10,... | collective-permute-start | bytes 884744 | tf_op jit(solution)/shard_map/ppermute | solution.py:33
  32.3 5.8 %collective-permute-start.10 = (bf16[400,1152]{1,0:T(8,128)(2,1)S(1)}, bf16[400,1152]{1,0:T(8,128)(2,1)S(1)}, u32[]{:S(2)}, u32[]{:S(2)}) collective-permute-start(bf16[400,1152]{1,0:T(8,128)(2,1)S(1)} %collective-permute-done.2.refs_0_.refs_2_), channel_id=1, source_target_pairs={{0,16},{16,0},{1,17},{17,1},{2,18},{18,2},{3,19},{19,3},{4,20},{20... | collective-permute-start | bytes 2764808 | tf_op jit(solution)/shard_map/ppermute | solution.py:37
  32.3 5.7 %collective-permute-start.11 = (bf16[128,1152]{1,0:T(8,128)(2,1)S(1)}, bf16[128,1152]{1,0:T(8,128)(2,1)S(1)}, u32[]{:S(2)}, u32[]{:S(2)}) collective-permute-start(bf16[128,1152]{1,0:T(8,128)(2,1)S(1)} %collective-permute-done.5.refs_1_), channel_id=1, source_target_pairs={{0,16},{16,0},{1,17},{17,1},{2,18},{18,2},{3,19},{19,3},{4,20},{20... | collective-permute-start | bytes 884744 | tf_op jit(solution)/shard_map/ppermute | solution.py:37
  33.0 13.7 %collective-permute-start.13 = (bf16[288,1152]{1,0:T(8,128)(2,1)S(1)}, bf16[288,1152]{1,0:T(8,128)(2,1)S(1)}, u32[]{:S(2)}, u32[]{:S(2)}) collective-permute-start(bf16[288,1152]{1,0:T(8,128)(2,1)S(1)} %pad_maximum_fusion), channel_id=1, source_target_pairs={{0,1},{1,0},{2,3},{3,2},{4,5},{5,4},{6,7},{7,6},{8,9},{9,8},{10,11... | collective-permute-start | bytes 1990664 | tf_op jit(solution)/shard_map/ppermute | solution.py:33
  34.9 21.2 %collective-permute-start.15 = (bf16[320,1152]{1,0:T(8,128)(2,1)S(1)}, bf16[320,1152]{1,0:T(8,128)(2,1)S(1)}, u32[]{:S(2)}, u32[]{:S(2)}) collective-permute-start(bf16[320,1152]{1,0:T(8,128)(2,1)S(1)} %slice_select_fusion), channel_id=1, source_target_pairs={{0,4},{1,5},{2,6},{3,7},{4,0},{5,1},{6,2},{7,3},{8,12},{9,13},{10,... | collective-permute-start | bytes 2211848 | tf_op jit(solution)/shard_map/ppermute | solution.py:33
  45.9 6.0 %collective-permute-start.12 = (bf16[144,768]{1,0:T(8,128)(2,1)S(1)}, bf16[144,768]{1,0:T(8,128)(2,1)S(1)}, u32[]{:S(2)}, u32[]{:S(2)}) collective-permute-start(bf16[144,768]{1,0:T(8,128)(2,1)S(1)} %get-tuple-element.51), channel_id=1, source_target_pairs={{0,1},{1,0},{2,3},{3,2},{4,5},{5,4},{6,7},{7,6},{8,9},{9,8},{10,11... | collective-permute-start | bytes 663560 | tf_op jit(solution)/shard_map/ppermute | solution.py:33
  51.9 10.0 %collective-permute-start.14 = (bf16[288,1152]{1,0:T(8,128)(2,1)S(1)}, bf16[288,1152]{1,0:T(8,128)(2,1)S(1)}, u32[]{:S(2)}, u32[]{:S(2)}) collective-permute-start(bf16[288,1152]{1,0:T(8,128)(2,1)S(1)} %collective-permute-done.13.refs_3_), channel_id=1, source_target_pairs={{0,16},{16,0},{1,17},{17,1},{2,18},{18,2},{3,19},{19,3},{4,20},{20... | collective-permute-start | bytes 1990664 | tf_op jit(solution)/shard_map/ppermute | solution.py:37
  54.4 6.6 %collective-permute-start.18 = (bf16[144,384]{1,0:T(8,128)(2,1)S(1)}, bf16[144,384]{1,0:T(8,128)(2,1)S(1)}, u32[]{:S(2)}, u32[]{:S(2)}) collective-permute-start(bf16[144,384]{1,0:T(8,128)(2,1)S(1)} %pad_maximum_fusion.9), channel_id=1, source_target_pairs={{0,6},{1,7},{2,4},{3,5},{4,2},{5,3},{6,0},{7,1},{8,14},{9,15},{10,... | collective-permute-start | bytes 331784 | tf_op jit(solution)/shard_map/ppermute | solution.py:33
  61.0 11.3 %collective-permute-start.19 = (bf16[176,1152]{1,0:T(8,128)(2,1)S(1)}, bf16[176,1152]{1,0:T(8,128)(2,1)S(1)}, u32[]{:S(2)}, u32[]{:S(2)}) collective-permute-start(bf16[176,1152]{1,0:T(8,128)(2,1)S(1)} %slice_select_fusion.1), channel_id=1, source_target_pairs={{0,4},{1,5},{2,6},{3,7},{4,0},{5,1},{6,2},{7,3},{8,12},{9,13},{10,... | collective-permute-start | bytes 1216520 | tf_op jit(solution)/shard_map/ppermute | solution.py:33
  61.9 13.7 %collective-permute-start.21 = (bf16[320,1152]{1,0:T(8,128)(2,1)S(1)}, bf16[320,1152]{1,0:T(8,128)(2,1)S(1)}, u32[]{:S(2)}, u32[]{:S(2)}) collective-permute-start(bf16[320,1152]{1,0:T(8,128)(2,1)S(1)} %collective-permute-done.15.refs_1_), channel_id=1, source_target_pairs={{0,16},{16,0},{1,17},{17,1},{2,18},{18,2},{3,19},{19,3},{4,20},{20... | collective-permute-start | bytes 2211848 | tf_op jit(solution)/shard_map/ppermute | solution.py:37
  63.8 8.4 %collective-permute-start.20 = (bf16[192,1152]{1,0:T(8,128)(2,1)S(1)}, bf16[192,1152]{1,0:T(8,128)(2,1)S(1)}, u32[]{:S(2)}, u32[]{:S(2)}) collective-permute-start(bf16[192,1152]{1,0:T(8,128)(2,1)S(1)} %get-tuple-element.66.refs_0_), channel_id=1, source_target_pairs={{0,1},{1,0},{2,3},{3,2},{4,5},{5,4},{6,7},{7,6},{8,9},{9,8},{10,11... | collective-permute-start | bytes 1327112 | tf_op jit(solution)/shard_map/ppermute | solution.py:33
  72.4 6.8 %collective-permute-start.23 = (bf16[128,1152]{1,0:T(8,128)(2,1)S(1)}, bf16[128,1152]{1,0:T(8,128)(2,1)S(1)}, u32[]{:S(2)}, u32[]{:S(2)}) collective-permute-start(bf16[128,1152]{1,0:T(8,128)(2,1)S(1)} %pad_maximum_fusion.3), channel_id=1, source_target_pairs={{0,2},{1,3},{2,0},{3,1},{4,6},{5,7},{6,4},{7,5},{8,10},{9,11},{10,... | collective-permute-start | bytes 884744 | tf_op jit(solution)/shard_map/ppermute | solution.py:33
  73.5 8.9 %collective-permute-start.24 = (bf16[128,1152]{1,0:T(8,128)(2,1)S(1)}, bf16[128,1152]{1,0:T(8,128)(2,1)S(1)}, u32[]{:S(2)}, u32[]{:S(2)}) collective-permute-start(bf16[128,1152]{1,0:T(8,128)(2,1)S(1)} %pad_maximum_fusion.4), channel_id=1, source_target_pairs={{0,2},{1,3},{2,0},{3,1},{4,6},{5,7},{6,4},{7,5},{8,10},{9,11},{10,... | collective-permute-start | bytes 884744 | tf_op jit(solution)/shard_map/ppermute | solution.py:33
  74.5 11.0 %collective-permute-start.25 = (bf16[128,1152]{1,0:T(8,128)(2,1)S(1)}, bf16[128,1152]{1,0:T(8,128)(2,1)S(1)}, u32[]{:S(2)}, u32[]{:S(2)}) collective-permute-start(bf16[128,1152]{1,0:T(8,128)(2,1)S(1)} %pad_maximum_fusion.5), channel_id=1, source_target_pairs={{0,2},{1,3},{2,0},{3,1},{4,6},{5,7},{6,4},{7,5},{8,10},{9,11},{10,... | collective-permute-start | bytes 884744 | tf_op jit(solution)/shard_map/ppermute | solution.py:33
  80.7 10.2 %collective-permute-start.26 = (bf16[128,1152]{1,0:T(8,128)(2,1)S(1)}, bf16[128,1152]{1,0:T(8,128)(2,1)S(1)}, u32[]{:S(2)}, u32[]{:S(2)}) collective-permute-start(bf16[128,1152]{1,0:T(8,128)(2,1)S(1)} %mlp_far0.1), channel_id=1, source_target_pairs={{0,2},{1,3},{2,0},{3,1},{4,6},{5,7},{6,4},{7,5},{8,10},{9,11},{10,... | collective-permute-start | bytes 884744 | tf_op jit(solution)/shard_map/ppermute | solution.py:33
  83.8 8.0 %collective-permute-start.27 = (bf16[128,1152]{1,0:T(8,128)(2,1)S(1)}, bf16[128,1152]{1,0:T(8,128)(2,1)S(1)}, u32[]{:S(2)}, u32[]{:S(2)}) collective-permute-start(bf16[128,1152]{1,0:T(8,128)(2,1)S(1)} %mlp_far1.1), channel_id=1, source_target_pairs={{0,2},{1,3},{2,0},{3,1},{4,6},{5,7},{6,4},{7,5},{8,10},{9,11},{10,... | collective-permute-start | bytes 884744 | tf_op jit(solution)/shard_map/ppermute | solution.py:33
  87.0 10.6 %collective-permute-start.28 = (bf16[128,1152]{1,0:T(8,128)(2,1)S(1)}, bf16[128,1152]{1,0:T(8,128)(2,1)S(1)}, u32[]{:S(2)}, u32[]{:S(2)}) collective-permute-start(bf16[128,1152]{1,0:T(8,128)(2,1)S(1)} %mlp_far2.1), channel_id=1, source_target_pairs={{0,2},{1,3},{2,0},{3,1},{4,6},{5,7},{6,4},{7,5},{8,10},{9,11},{10,... | collective-permute-start | bytes 884744 | tf_op jit(solution)/shard_map/ppermute | solution.py:33
  90.9 6.8 %collective-permute-start.29 = (bf16[64,1152]{1,0:T(8,128)(2,1)S(1)}, bf16[64,1152]{1,0:T(8,128)(2,1)S(1)}, u32[]{:S(2)}, u32[]{:S(2)}) collective-permute-start(bf16[64,1152]{1,0:T(8,128)(2,1)S(1)} %add_convert_fusion.2), channel_id=1, source_target_pairs={{0,1},{1,0},{2,3},{3,2},{4,5},{5,4},{6,7},{7,6},{8,9},{9,8},{10,11... | collective-permute-start | bytes 442376 | tf_op jit(solution)/shard_map/ppermute | solution.py:33
  91.9 5.8 %collective-permute-start.30 = (bf16[64,1152]{1,0:T(8,128)(2,1)S(1)}, bf16[64,1152]{1,0:T(8,128)(2,1)S(1)}, u32[]{:S(2)}, u32[]{:S(2)}) collective-permute-start(bf16[64,1152]{1,0:T(8,128)(2,1)S(1)} %add_convert_fusion.1), channel_id=1, source_target_pairs={{0,1},{1,0},{2,3},{3,2},{4,5},{5,4},{6,7},{7,6},{8,9},{9,8},{10,11... | collective-permute-start | bytes 442376 | tf_op jit(solution)/shard_map/ppermute | solution.py:33
  (20 other events, 121.6 us)
where the time goes:
time: 107 us
  waiting for transfers between devices  44.3 us (41%)
  starting transfers between devices  29.6 us (28%)
  Pallas kernels  26.8 us (25%)
  other arithmetic  2.38 us (2%)
  local copies, waits for them, and re-layouts  2.37 us (2%)
  between operations  1.08 us (1%)
    ppermute x23, waiting for transfers between devices, permute_by(): return lax.ppermute(block, ('cfg', 'tok'), route)  41.7 us
    ppermute x23, starting transfers between devices, permute_by(): return lax.ppermute(block, ('cfg', 'tok'), route)  27.9 us
    pallas_call x12, Pallas kernels, call(): pl.pallas_call(kernel, out_shape=out_shape, in_specs=specs or [whole] * l...  26.8 us
    ppermute x10, waiting for transfers between devices, from_other_half(): return lax.ppermute(block, 'cfg', [(0, 1), (1, 0)])  2.65 us
  transfers between devices with their start and end apart: 33, of which 18 were waited for; matrix products, arithmetic and copies ran while one was open for 4% of the time, Pallas kernels for 22%

commit v1 on v0

--- a/solution.py
+++ b/solution.py
@@ -461,6 +461,7 @@
     hidden = up_t.shape[0]
     cuts = (0, FAR_EARLY[0], sum(FAR_EARLY), hidden)
     large_rows, small_rows = first_payloads(hidden_in, up_t, down_t, large, small, cuts[1])
+    own_rows = after(lax.dynamic_slice_in_dim(after(hidden_in, large_rows), core * half, half))
     proj_rows = None
     got, away = [], []
     for step in range(3):
@@ -493,6 +494,8 @@
                 (got_large, got_small, early, *sent)
             )
             proj_rows = jnp.concatenate([proj_rows, got_large[4 * large :]])
+        if step == 0:
+            large_rows, small_rows = own_rows[:large], own_rows[large:]
         if step < 2:
             large_rows = jnp.concatenate([large_rows, got_large[: large << step]])
             small_rows = jnp.concatenate([rows[: small << step] for rows in (small_rows, got_small)])

time: 107 us -> 108 us (level)
  local copies, waits for them, and re-layouts: 2.37 us -> 3.88 us
  transfers between devices with their start and end apart: 33 -> 33, of which waited for: 18 -> 19; matrix products, arithmetic and copies ran while one was open for 4% -> 4% of each run, Pallas kernels for 22% -> 21%
where the time goes in v1:
time: 108 us
  waiting for transfers between devices  44.8 us (41%)
  starting transfers between devices  29.9 us (28%)
  Pallas kernels  26.8 us (25%)
  local copies, waits for them, and re-layouts  3.88 us (4%)
  other arithmetic  1.33 us (1%)
    ppermute x23, waiting for transfers between devices, permute_by(): return lax.ppermute(block, ('cfg', 'tok'), route)  42.2 us
    ppermute x23, starting transfers between devices, permute_by(): return lax.ppermute(block, ('cfg', 'tok'), route)  28.1 us
    pallas_call x12, Pallas kernels, call(): pl.pallas_call(kernel, out_shape=out_shape, in_specs=specs or [whole] * l...  26.8 us
    ppermute x10, waiting for transfers between devices, from_other_half(): return lax.ppermute(block, 'cfg', [(0, 1), (1, 0)])  2.65 us
  transfers between devices with their start and end apart: 33, of which 19 were waited for; matrix products, arithmetic and copies ran while one was open for 4% of the time, Pallas kernels for 21%

profile of v1, /device:TPU:0, one launch (start us, length us, event | category | flops | bytes accessed | tf_op | source)
XLA Modules:
  0.0 107.7 jit_solution(244699334985051518)
XLA Ops:
  0.6 1.9 %first.1 = (bf16[64,1152]{1,0:T(8,128)(2,1)}, bf16[112,1152]{1,0:T(8,128)(2,1)}) custom-call(bf16[192,1152]{1,0:T(8,128)(2,1)} %hidden_ref.3, bf16[576,1152]{1,0:T(8,128)(2,1)} %bitcast.23, bf16[576,1152]{1,0:T(8,128)(2,1)} %bitcast.27), custom_call_target="tpu_custom_call" | custom-call | bytes 3096576 | tf_op jit(solution)/shard_map/first/pallas_call | solution.py:62
  2.5 3.0 %collective-permute-start = (bf16[64,1152]{1,0:T(8,128)(2,1)}, bf16[64,1152]{1,0:T(8,128)(2,1)S(1)}, u32[]{:S(2)}, u32[]{:S(2)}) collective-permute-start(bf16[64,1152]{1,0:T(8,128)(2,1)} %get-tuple-element.39), channel_id=1, source_target_pairs={{0,1},{1,0},{2,3},{3,2},{4,5},{5,4},{6,7},{7,6},{8,9},{9,8},{10,11... | collective-permute-start | bytes 442376 | tf_op jit(solution)/shard_map/ppermute | solution.py:33
  8.9 2.1 %collective-permute-start.1 = (bf16[200,1152]{1,0:T(8,128)(2,1)S(1)}, bf16[200,1152]{1,0:T(8,128)(2,1)S(1)}, u32[]{:S(2)}, u32[]{:S(2)}) collective-permute-start(bf16[200,1152]{1,0:T(8,128)(2,1)S(1)} %pad_maximum_fusion.1), channel_id=1, source_target_pairs={{0,2},{1,3},{2,0},{3,1},{4,6},{5,7},{6,4},{7,5},{8,10},{9,11},{10,... | collective-permute-start | bytes 1382408 | tf_op jit(solution)/shard_map/ppermute | solution.py:33
  11.7 3.2 %collective-permute-done.3.refs_3_.refs_0_ = bf16[112,1152]{1,0:T(8,128)(2,1)S(1)} collective-permute-done((bf16[112,1152]{1,0:T(8,128)(2,1)}, bf16[112,1152]{1,0:T(8,128)(2,1)S(1)}, u32[]{:S(2)}, u32[]{:S(2)}) %collective-permute-start.3) | collective-permute-done | bytes 258080 | tf_op jit(solution)/shard_map/ppermute | solution.py:33
  15.0 2.5 %collective-permute-done.1.refs_2_.refs_1_ = bf16[200,1152]{1,0:T(8,128)(2,1)S(1)} collective-permute-done((bf16[200,1152]{1,0:T(8,128)(2,1)S(1)}, bf16[200,1152]{1,0:T(8,128)(2,1)S(1)}, u32[]{:S(2)}, u32[]{:S(2)}) %collective-permute-start.1) | collective-permute-done | bytes 460832 | tf_op jit(solution)/shard_map/ppermute | solution.py:33
  19.6 2.1 %collective-permute-start.2 = (bf16[400,1152]{1,0:T(8,128)(2,1)}, bf16[400,1152]{1,0:T(8,128)(2,1)S(1)}, u32[]{:S(2)}, u32[]{:S(2)}) collective-permute-start(bf16[400,1152]{1,0:T(8,128)(2,1)} %get-tuple-element.77), channel_id=1, source_target_pairs={{0,4},{1,5},{2,6},{3,7},{4,0},{5,1},{6,2},{7,3},{8,12},{9,13},{10,... | collective-permute-start | bytes 2764808 | tf_op jit(solution)/shard_map/ppermute | solution.py:33
  26.0 2.5 %qkv_early.1 = (bf16[768,768]{1,0:T(8,128)(2,1)S(1)}, bf16[768,1152]{1,0:T(8,128)(2,1)S(1)}) custom-call(f32[2,8,1152]{2,1,0:T(8,128)S(1)} %bitcast.31, bf16[432,1152]{1,0:T(8,128)(2,1)S(1)} %bitcast.38, bf16[192,1152]{1,0:T(8,128)(2,1)S(1)} %copy-done.2, bf16[64,1152]{1,0:T(8,128)(2,1)S(1)} %collective-permute-done.refs_1_, ...), custom_call_target="tpu_custom_call" | custom-call | flops 1358954496 | bytes 3538944 | tf_op jit(solution)/shard_map/qkv_early/pallas_call | solution.py:62
  28.6 2.9 %collective-permute-done.5.refs_1_ = bf16[128,1152]{1,0:T(8,128)(2,1)S(1)} collective-permute-done((bf16[128,1152]{1,0:T(8,128)(2,1)S(1)}, bf16[128,1152]{1,0:T(8,128)(2,1)S(1)}, u32[]{:S(2)}, u32[]{:S(2)}) %collective-permute-start.5) | collective-permute-done | bytes 294944 | tf_op jit(solution)/shard_map/ppermute | solution.py:33
  31.5 1.8 %collective-permute-done.2.refs_0_.refs_2_ = bf16[400,1152]{1,0:T(8,128)(2,1)S(1)} collective-permute-done((bf16[400,1152]{1,0:T(8,128)(2,1)}, bf16[400,1152]{1,0:T(8,128)(2,1)S(1)}, u32[]{:S(2)}, u32[]{:S(2)}) %collective-permute-start.2) | collective-permute-done | bytes 921632 | tf_op jit(solution)/shard_map/ppermute | solution.py:33
  34.0 2.0 %collective-permute-start.13 = (bf16[288,1152]{1,0:T(8,128)(2,1)S(1)}, bf16[288,1152]{1,0:T(8,128)(2,1)S(1)}, u32[]{:S(2)}, u32[]{:S(2)}) collective-permute-start(bf16[288,1152]{1,0:T(8,128)(2,1)S(1)} %pad_maximum_fusion), channel_id=1, source_target_pairs={{0,1},{1,0},{2,3},{3,2},{4,5},{5,4},{6,7},{7,6},{8,9},{9,8},{10,11... | collective-permute-start | bytes 1990664 | tf_op jit(solution)/shard_map/ppermute | solution.py:33
  37.6 1.6 %qkv_late_own.1.refs_0_ = bf16[384,768]{1,0:T(8,128)(2,1)S(1)} custom-call(f32[2,8,1152]{2,1,0:T(8,128)S(1)} %bitcast.32, bf16[768,1152]{1,0:T(8,128)(2,1)S(1)} %get-tuple-element.48.weight_ref, bf16[400,1152]{1,0:T(8,128)(2,1)S(1)} %collective-permute-done.2.refs_0_.refs_2_, bf16[128,1152]{1,0:T(8,128)(2,1)S(1)} %collective-permute-done.5.refs_1_), custom_call_target="tpu_custom_call" | custom-call | flops 679477248 | bytes 3059712 | tf_op jit(solution)/shard_map/qkv_late_own/pallas_call | solution.py:62
  39.2 1.6 %qkv_late_other.1.refs_1_ = bf16[384,768]{1,0:T(8,128)(2,1)S(1)} custom-call(f32[2,8,1152]{2,1,0:T(8,128)S(1)} %bitcast.33, bf16[768,1152]{1,0:T(8,128)(2,1)S(1)} %get-tuple-element.48.weight_ref, bf16[400,1152]{1,0:T(8,128)(2,1)S(1)} %collective-permute-done.10.refs_0_.refs_6_, bf16[128,1152]{1,0:T(8,128)(2,1)S(1)} %collective-permute-done.11.refs_1_), custom_call_target="tpu_custom_call" | custom-call | flops 679477248 | bytes 3059712 | tf_op jit(solution)/shard_map/qkv_late_other/pallas_call | solution.py:62
  40.8 6.2 %attend.1 = (bf16[144,768]{1,0:T(8,128)(2,1)S(1)}, bf16[144,768]{1,0:T(8,128)(2,1)S(1)}) custom-call(s32[2,8]{1,0:T(2,128)S(1)} %copy-done.6, bf16[768,768]{1,0:T(8,128)(2,1)S(1)} %get-tuple-element.45.early_ref, bf16[384,768]{1,0:T(8,128)(2,1)S(1)} %qkv_late_own.1.refs_0_, bf16[384,768]{1,0:T(8,128)(2,1)S(1)} %qkv_late_other.1.refs_1_), custom_call_target="tpu_custom_call" | custom-call | flops 1358954496 | bytes 2359360 | tf_op jit(solution)/shard_map/attend/pallas_call | solution.py:62
  47.8 5.3 %collective-permute-done.12.mate_ref = bf16[144,768]{1,0:T(8,128)(2,1)S(1)} collective-permute-done((bf16[144,768]{1,0:T(8,128)(2,1)S(1)}, bf16[144,768]{1,0:T(8,128)(2,1)S(1)}, u32[]{:S(2)}, u32[]{:S(2)}) %collective-permute-start.12) | collective-permute-done | bytes 221216 | tf_op jit(solution)/shard_map/ppermute | solution.py:33
  58.1 2.4 %collective-permute-done.17.refs_9_ = bf16[144,384]{1,0:T(8,128)(2,1)S(1)} collective-permute-done((bf16[144,384]{1,0:T(8,128)(2,1)S(1)}, bf16[144,384]{1,0:T(8,128)(2,1)S(1)}, u32[]{:S(2)}, u32[]{:S(2)}) %collective-permute-start.17) | collective-permute-done | bytes 110624 | tf_op jit(solution)/shard_map/ppermute | solution.py:33
  60.5 1.7 %collective-permute-done.18.refs_10_ = bf16[144,384]{1,0:T(8,128)(2,1)S(1)} collective-permute-done((bf16[144,384]{1,0:T(8,128)(2,1)S(1)}, bf16[144,384]{1,0:T(8,128)(2,1)S(1)}, u32[]{:S(2)}, u32[]{:S(2)}) %collective-permute-start.18) | collective-permute-done | bytes 110624 | tf_op jit(solution)/shard_map/ppermute | solution.py:33
  63.0 1.9 %project.1 = (f32[192,1152]{1,0:T(8,128)S(1)}, bf16[192,1152]{1,0:T(8,128)(2,1)S(1)}) custom-call(f32[2,8,1152]{2,1,0:T(8,128)S(1)} %bitcast.34, bf16[192,1152]{1,0:T(8,128)(2,1)S(1)} %copy-done.2, bf16[144,768]{1,0:T(8,128)(2,1)S(1)} %get-tuple-element.52.mine_ref, bf16[144,768]{1,0:T(8,128)(2,1)S(1)} %collective-permute-done.12.mate_ref, ...), custom_call_target="tpu_custom_call" | custom-call | flops 509607936 | bytes 5713920 | tf_op jit(solution)/shard_map/project/pallas_call | solution.py:62
  65.6 7.7 %collective-permute-done.20.refs_1_ = bf16[192,1152]{1,0:T(8,128)(2,1)S(1)} collective-permute-done((bf16[192,1152]{1,0:T(8,128)(2,1)S(1)}, bf16[192,1152]{1,0:T(8,128)(2,1)S(1)}, u32[]{:S(2)}, u32[]{:S(2)}) %collective-permute-start.20) | collective-permute-done | bytes 442400 | tf_op jit(solution)/shard_map/ppermute | solution.py:33
  76.7 2.0 %pack.1 = (bf16[1152,1152]{1,0:T(8,128)(2,1)S(1)}, bf16[1152,1152]{1,0:T(8,128)(2,1)S(1)}) custom-call(bf16[576,1152]{1,0:T(8,128)(2,1)S(1)} %bitcast.26, bf16[576,1152]{1,0:T(8,128)(2,1)S(1)} %bitcast.30, bf16[112,1152]{1,0:T(8,128)(2,1)S(1)} %collective-permute-done.3.refs_3_.refs_0_, bf16[320,1152]{1,0:T(8,128)(2,1)S(1)} %collective-permute-done.15.refs_1_, ...), custom_call_target="tpu_custom_call" | custom-call | bytes 5455872 | tf_op jit(solution)/shard_map/pack/pallas_call | solution.py:62
  78.7 1.6 %collective-permute-done.23.refs_0_ = bf16[128,1152]{1,0:T(8,128)(2,1)S(1)} collective-permute-done((bf16[128,1152]{1,0:T(8,128)(2,1)S(1)}, bf16[128,1152]{1,0:T(8,128)(2,1)S(1)}, u32[]{:S(2)}, u32[]{:S(2)}) %collective-permute-start.23) | collective-permute-done | bytes 294944 | tf_op jit(solution)/shard_map/ppermute | solution.py:33
  89.2 2.7 %mlp_near.1 = (f32[192,1152]{1,0:T(8,128)S(1)}, f32[64,1152]{1,0:T(8,128)S(1)}, f32[64,1152]{1,0:T(8,128)S(1)}, f32[64,1152]{1,0:T(8,128)S(1)}) custom-call(bf16[1152,1152]{1,0:T(8,128)(2,1)S(1)} %get-tuple-element.66.up_ref, bf16[1152,1152]{1,0:T(8,128)(2,1)S(1)} %get-tuple-element.67.down_ref, bf16[192,1152]{1,0:T(8,128)(2,1)S(1)} %get-tuple-element.68.refs_0_, ...), custom_call_target="tpu_custom_call" | custom-call | flops 2038431744 | bytes 6193152 | tf_op jit(solution)/shard_map/mlp_near/pallas_call | solution.py:62
  94.3 4.5 %collective-permute-done.28.refs_2_ = bf16[128,1152]{1,0:T(8,128)(2,1)S(1)} collective-permute-done((bf16[128,1152]{1,0:T(8,128)(2,1)S(1)}, bf16[128,1152]{1,0:T(8,128)(2,1)S(1)}, u32[]{:S(2)}, u32[]{:S(2)}) %collective-permute-start.28) | collective-permute-done | bytes 294944 | tf_op jit(solution)/shard_map/ppermute | solution.py:33
  98.9 5.1 %collective-permute-done.31.refs_5_ = bf16[64,1152]{1,0:T(8,128)(2,1)S(1)} collective-permute-done((bf16[64,1152]{1,0:T(8,128)(2,1)S(1)}, bf16[64,1152]{1,0:T(8,128)(2,1)S(1)}, u32[]{:S(2)}, u32[]{:S(2)}) %collective-permute-start.31) | collective-permute-done | bytes 147488 | tf_op jit(solution)/shard_map/ppermute | solution.py:33
  104.0 1.9 %finish.1 = (bf16[192,1152]{1,0:T(8,128)(2,1)}, f32[16,192]{1,0:T(8,128)S(1)}, f32[16,192]{1,0:T(8,128)S(1)}) custom-call(s32[2,8]{1,0:T(2,128)S(1)} %copy-done.6, f32[2]{0:T(128)S(1)} %copy-done.8, f32[2,2]{1,0:T(2,128)S(1)} %copy-done.7, f32[2,8,1152]{2,1,0:T(8,128)S(1)} %bitcast.35, f32[192,1152]{1,0:T(8,128)S(1)} %get-tuple-element.60.mid_ref, ...), custom_call_target="tpu_custom_call" | custom-call | flops 7077888 | bytes 3219544 | tf_op jit(solution)/shard_map/finish/pallas_call | solution.py:62
  (106 shorter events, 36.4 us)
Async XLA Ops:
  2.5 6.3 %collective-permute-start = (bf16[64,1152]{1,0:T(8,128)(2,1)}, bf16[64,1152]{1,0:T(8,128)(2,1)S(1)}, u32[]{:S(2)}, u32[]{:S(2)}) collective-permute-start(bf16[64,1152]{1,0:T(8,128)(2,1)} %get-tuple-element.39), channel_id=1, source_target_pairs={{0,1},{1,0},{2,3},{3,2},{4,5},{5,4},{6,7},{7,6},{8,9},{9,8},{10,11... | collective-permute-start | bytes 442376 | tf_op jit(solution)/shard_map/ppermute | solution.py:33
  5.5 9.3 %collective-permute-start.3 = (bf16[112,1152]{1,0:T(8,128)(2,1)}, bf16[112,1152]{1,0:T(8,128)(2,1)S(1)}, u32[]{:S(2)}, u32[]{:S(2)}) collective-permute-start(bf16[112,1152]{1,0:T(8,128)(2,1)} %get-tuple-element.41), channel_id=1, source_target_pairs={{0,4},{1,5},{2,6},{3,7},{4,0},{5,1},{6,2},{7,3},{8,12},{9,13},{10,... | collective-permute-start | bytes 774152 | tf_op jit(solution)/shard_map/ppermute | solution.py:33
  8.9 8.6 %collective-permute-start.1 = (bf16[200,1152]{1,0:T(8,128)(2,1)S(1)}, bf16[200,1152]{1,0:T(8,128)(2,1)S(1)}, u32[]{:S(2)}, u32[]{:S(2)}) collective-permute-start(bf16[200,1152]{1,0:T(8,128)(2,1)S(1)} %pad_maximum_fusion.1), channel_id=1, source_target_pairs={{0,2},{1,3},{2,0},{3,1},{4,6},{5,7},{6,4},{7,5},{8,10},{9,11},{10,... | collective-permute-start | bytes 1382408 | tf_op jit(solution)/shard_map/ppermute | solution.py:33
  14.9 7.5 %collective-permute-start.4 = (bf16[64,1152]{1,0:T(8,128)(2,1)S(1)}, bf16[64,1152]{1,0:T(8,128)(2,1)S(1)}, u32[]{:S(2)}, u32[]{:S(2)}) collective-permute-start(bf16[64,1152]{1,0:T(8,128)(2,1)S(1)} %pad_maximum_fusion.6), channel_id=1, source_target_pairs={{0,1},{1,0},{2,3},{3,2},{4,5},{5,4},{6,7},{7,6},{8,9},{9,8},{10,11... | collective-permute-start | bytes 442376 | tf_op jit(solution)/shard_map/ppermute | solution.py:33
  19.6 13.7 %collective-permute-start.2 = (bf16[400,1152]{1,0:T(8,128)(2,1)}, bf16[400,1152]{1,0:T(8,128)(2,1)S(1)}, u32[]{:S(2)}, u32[]{:S(2)}) collective-permute-start(bf16[400,1152]{1,0:T(8,128)(2,1)} %get-tuple-element.77), channel_id=1, source_target_pairs={{0,4},{1,5},{2,6},{3,7},{4,0},{5,1},{6,2},{7,3},{8,12},{9,13},{10,... | collective-permute-start | bytes 2764808 | tf_op jit(solution)/shard_map/ppermute | solution.py:33
  22.4 9.1 %collective-permute-start.5 = (bf16[128,1152]{1,0:T(8,128)(2,1)S(1)}, bf16[128,1152]{1,0:T(8,128)(2,1)S(1)}, u32[]{:S(2)}, u32[]{:S(2)}) collective-permute-start(bf16[128,1152]{1,0:T(8,128)(2,1)S(1)} %pad_maximum_fusion.2), channel_id=1, source_target_pairs={{0,2},{1,3},{2,0},{3,1},{4,6},{5,7},{6,4},{7,5},{8,10},{9,11},{10,... | collective-permute-start | bytes 884744 | tf_op jit(solution)/shard_map/ppermute | solution.py:33
  33.3 5.9 %collective-permute-start.10 = (bf16[400,1152]{1,0:T(8,128)(2,1)S(1)}, bf16[400,1152]{1,0:T(8,128)(2,1)S(1)}, u32[]{:S(2)}, u32[]{:S(2)}) collective-permute-start(bf16[400,1152]{1,0:T(8,128)(2,1)S(1)} %collective-permute-done.2.refs_0_.refs_2_), channel_id=1, source_target_pairs={{0,16},{16,0},{1,17},{17,1},{2,18},{18,2},{3,19},{19,3},{4,20},{20... | collective-permute-start | bytes 2764808 | tf_op jit(solution)/shard_map/ppermute | solution.py:37
  33.4 5.8 %collective-permute-start.11 = (bf16[128,1152]{1,0:T(8,128)(2,1)S(1)}, bf16[128,1152]{1,0:T(8,128)(2,1)S(1)}, u32[]{:S(2)}, u32[]{:S(2)}) collective-permute-start(bf16[128,1152]{1,0:T(8,128)(2,1)S(1)} %collective-permute-done.5.refs_1_), channel_id=1, source_target_pairs={{0,16},{16,0},{1,17},{17,1},{2,18},{18,2},{3,19},{19,3},{4,20},{20... | collective-permute-start | bytes 884744 | tf_op jit(solution)/shard_map/ppermute | solution.py:37
  34.0 13.8 %collective-permute-start.13 = (bf16[288,1152]{1,0:T(8,128)(2,1)S(1)}, bf16[288,1152]{1,0:T(8,128)(2,1)S(1)}, u32[]{:S(2)}, u32[]{:S(2)}) collective-permute-start(bf16[288,1152]{1,0:T(8,128)(2,1)S(1)} %pad_maximum_fusion), channel_id=1, source_target_pairs={{0,1},{1,0},{2,3},{3,2},{4,5},{5,4},{6,7},{7,6},{8,9},{9,8},{10,11... | collective-permute-start | bytes 1990664 | tf_op jit(solution)/shard_map/ppermute | solution.py:33
  36.0 21.2 %collective-permute-start.15 = (bf16[320,1152]{1,0:T(8,128)(2,1)S(1)}, bf16[320,1152]{1,0:T(8,128)(2,1)S(1)}, u32[]{:S(2)}, u32[]{:S(2)}) collective-permute-start(bf16[320,1152]{1,0:T(8,128)(2,1)S(1)} %slice_select_fusion), channel_id=1, source_target_pairs={{0,4},{1,5},{2,6},{3,7},{4,0},{5,1},{6,2},{7,3},{8,12},{9,13},{10,... | collective-permute-start | bytes 2211848 | tf_op jit(solution)/shard_map/ppermute | solution.py:33
  47.1 6.0 %collective-permute-start.12 = (bf16[144,768]{1,0:T(8,128)(2,1)S(1)}, bf16[144,768]{1,0:T(8,128)(2,1)S(1)}, u32[]{:S(2)}, u32[]{:S(2)}) collective-permute-start(bf16[144,768]{1,0:T(8,128)(2,1)S(1)} %get-tuple-element.53), channel_id=1, source_target_pairs={{0,1},{1,0},{2,3},{3,2},{4,5},{5,4},{6,7},{7,6},{8,9},{9,8},{10,11... | collective-permute-start | bytes 663560 | tf_op jit(solution)/shard_map/ppermute | solution.py:33
  53.1 10.0 %collective-permute-start.14 = (bf16[288,1152]{1,0:T(8,128)(2,1)S(1)}, bf16[288,1152]{1,0:T(8,128)(2,1)S(1)}, u32[]{:S(2)}, u32[]{:S(2)}) collective-permute-start(bf16[288,1152]{1,0:T(8,128)(2,1)S(1)} %collective-permute-done.13.refs_3_), channel_id=1, source_target_pairs={{0,16},{16,0},{1,17},{17,1},{2,18},{18,2},{3,19},{19,3},{4,20},{20... | collective-permute-start | bytes 1990664 | tf_op jit(solution)/shard_map/ppermute | solution.py:37
  55.6 6.6 %collective-permute-start.18 = (bf16[144,384]{1,0:T(8,128)(2,1)S(1)}, bf16[144,384]{1,0:T(8,128)(2,1)S(1)}, u32[]{:S(2)}, u32[]{:S(2)}) collective-permute-start(bf16[144,384]{1,0:T(8,128)(2,1)S(1)} %pad_maximum_fusion.9), channel_id=1, source_target_pairs={{0,6},{1,7},{2,4},{3,5},{4,2},{5,3},{6,0},{7,1},{8,14},{9,15},{10,... | collective-permute-start | bytes 331784 | tf_op jit(solution)/shard_map/ppermute | solution.py:33
  62.1 11.3 %collective-permute-start.19 = (bf16[176,1152]{1,0:T(8,128)(2,1)S(1)}, bf16[176,1152]{1,0:T(8,128)(2,1)S(1)}, u32[]{:S(2)}, u32[]{:S(2)}) collective-permute-start(bf16[176,1152]{1,0:T(8,128)(2,1)S(1)} %slice_select_fusion.1), channel_id=1, source_target_pairs={{0,4},{1,5},{2,6},{3,7},{4,0},{5,1},{6,2},{7,3},{8,12},{9,13},{10,... | collective-permute-start | bytes 1216520 | tf_op jit(solution)/shard_map/ppermute | solution.py:33
  63.0 13.7 %collective-permute-start.21 = (bf16[320,1152]{1,0:T(8,128)(2,1)S(1)}, bf16[320,1152]{1,0:T(8,128)(2,1)S(1)}, u32[]{:S(2)}, u32[]{:S(2)}) collective-permute-start(bf16[320,1152]{1,0:T(8,128)(2,1)S(1)} %collective-permute-done.15.refs_1_), channel_id=1, source_target_pairs={{0,16},{16,0},{1,17},{17,1},{2,18},{18,2},{3,19},{19,3},{4,20},{20... | collective-permute-start | bytes 2211848 | tf_op jit(solution)/shard_map/ppermute | solution.py:37
  65.0 8.4 %collective-permute-start.20 = (bf16[192,1152]{1,0:T(8,128)(2,1)S(1)}, bf16[192,1152]{1,0:T(8,128)(2,1)S(1)}, u32[]{:S(2)}, u32[]{:S(2)}) collective-permute-start(bf16[192,1152]{1,0:T(8,128)(2,1)S(1)} %get-tuple-element.68.refs_0_), channel_id=1, source_target_pairs={{0,1},{1,0},{2,3},{3,2},{4,5},{5,4},{6,7},{7,6},{8,9},{9,8},{10,11... | collective-permute-start | bytes 1327112 | tf_op jit(solution)/shard_map/ppermute | solution.py:33
  73.6 6.8 %collective-permute-start.23 = (bf16[128,1152]{1,0:T(8,128)(2,1)S(1)}, bf16[128,1152]{1,0:T(8,128)(2,1)S(1)}, u32[]{:S(2)}, u32[]{:S(2)}) collective-permute-start(bf16[128,1152]{1,0:T(8,128)(2,1)S(1)} %pad_maximum_fusion.3), channel_id=1, source_target_pairs={{0,2},{1,3},{2,0},{3,1},{4,6},{5,7},{6,4},{7,5},{8,10},{9,11},{10,... | collective-permute-start | bytes 884744 | tf_op jit(solution)/shard_map/ppermute | solution.py:33
  74.7 8.8 %collective-permute-start.24 = (bf16[128,1152]{1,0:T(8,128)(2,1)S(1)}, bf16[128,1152]{1,0:T(8,128)(2,1)S(1)}, u32[]{:S(2)}, u32[]{:S(2)}) collective-permute-start(bf16[128,1152]{1,0:T(8,128)(2,1)S(1)} %pad_maximum_fusion.4), channel_id=1, source_target_pairs={{0,2},{1,3},{2,0},{3,1},{4,6},{5,7},{6,4},{7,5},{8,10},{9,11},{10,... | collective-permute-start | bytes 884744 | tf_op jit(solution)/shard_map/ppermute | solution.py:33
  75.7 11.0 %collective-permute-start.25 = (bf16[128,1152]{1,0:T(8,128)(2,1)S(1)}, bf16[128,1152]{1,0:T(8,128)(2,1)S(1)}, u32[]{:S(2)}, u32[]{:S(2)}) collective-permute-start(bf16[128,1152]{1,0:T(8,128)(2,1)S(1)} %pad_maximum_fusion.5), channel_id=1, source_target_pairs={{0,2},{1,3},{2,0},{3,1},{4,6},{5,7},{6,4},{7,5},{8,10},{9,11},{10,... | collective-permute-start | bytes 884744 | tf_op jit(solution)/shard_map/ppermute | solution.py:33
  81.8 10.2 %collective-permute-start.26 = (bf16[128,1152]{1,0:T(8,128)(2,1)S(1)}, bf16[128,1152]{1,0:T(8,128)(2,1)S(1)}, u32[]{:S(2)}, u32[]{:S(2)}) collective-permute-start(bf16[128,1152]{1,0:T(8,128)(2,1)S(1)} %mlp_far0.1), channel_id=1, source_target_pairs={{0,2},{1,3},{2,0},{3,1},{4,6},{5,7},{6,4},{7,5},{8,10},{9,11},{10,... | collective-permute-start | bytes 884744 | tf_op jit(solution)/shard_map/ppermute | solution.py:33
  85.0 8.0 %collective-permute-start.27 = (bf16[128,1152]{1,0:T(8,128)(2,1)S(1)}, bf16[128,1152]{1,0:T(8,128)(2,1)S(1)}, u32[]{:S(2)}, u32[]{:S(2)}) collective-permute-start(bf16[128,1152]{1,0:T(8,128)(2,1)S(1)} %mlp_far1.1), channel_id=1, source_target_pairs={{0,2},{1,3},{2,0},{3,1},{4,6},{5,7},{6,4},{7,5},{8,10},{9,11},{10,... | collective-permute-start | bytes 884744 | tf_op jit(solution)/shard_map/ppermute | solution.py:33
  88.1 10.6 %collective-permute-start.28 = (bf16[128,1152]{1,0:T(8,128)(2,1)S(1)}, bf16[128,1152]{1,0:T(8,128)(2,1)S(1)}, u32[]{:S(2)}, u32[]{:S(2)}) collective-permute-start(bf16[128,1152]{1,0:T(8,128)(2,1)S(1)} %mlp_far2.1), channel_id=1, source_target_pairs={{0,2},{1,3},{2,0},{3,1},{4,6},{5,7},{6,4},{7,5},{8,10},{9,11},{10,... | collective-permute-start | bytes 884744 | tf_op jit(solution)/shard_map/ppermute | solution.py:33
  92.1 6.8 %collective-permute-start.29 = (bf16[64,1152]{1,0:T(8,128)(2,1)S(1)}, bf16[64,1152]{1,0:T(8,128)(2,1)S(1)}, u32[]{:S(2)}, u32[]{:S(2)}) collective-permute-start(bf16[64,1152]{1,0:T(8,128)(2,1)S(1)} %add_convert_fusion.2), channel_id=1, source_target_pairs={{0,1},{1,0},{2,3},{3,2},{4,5},{5,4},{6,7},{7,6},{8,9},{9,8},{10,11... | collective-permute-start | bytes 442376 | tf_op jit(solution)/shard_map/ppermute | solution.py:33
  93.0 5.8 %collective-permute-start.30 = (bf16[64,1152]{1,0:T(8,128)(2,1)S(1)}, bf16[64,1152]{1,0:T(8,128)(2,1)S(1)}, u32[]{:S(2)}, u32[]{:S(2)}) collective-permute-start(bf16[64,1152]{1,0:T(8,128)(2,1)S(1)} %add_convert_fusion.1), channel_id=1, source_target_pairs={{0,1},{1,0},{2,3},{3,2},{4,5},{5,4},{6,7},{7,6},{8,9},{9,8},{10,11... | collective-permute-start | bytes 442376 | tf_op jit(solution)/shard_map/ppermute | solution.py:33
  (20 other events, 125.6 us)

commit v2 on v0

--- a/solution.py
+++ b/solution.py
@@ -18,7 +18,7 @@
 PROJ = ((2, 4, 1), (4, 1, 2))
 HEADS_TO = ((2, 4, 1), (4, 1, 2))
 FAR_EARLY = (80, 320)
-CHUNKS = 3
+CHUNKS = 4
 F32 = jnp.float32
 BF16 = jnp.bfloat16
 

time: 107 us -> 106 us (level)
  waiting for transfers between devices: 44.3 us -> 39.2 us
  starting transfers between devices: 29.6 us -> 32.6 us
  Pallas kernels: 26.8 us -> 28.2 us
    ppermute x23 -> x26, waiting for transfers between devices: 41.7 us -> 36.5 us  [permute_by(): return lax.ppermute(block, ('cfg', 'tok'), route)]
    ppermute x23 -> x26, starting transfers between devices: 27.9 us -> 30.8 us  [permute_by(): return lax.ppermute(block, ('cfg', 'tok'), route)]
    pallas_call x12 -> x13, Pallas kernels: 26.8 us -> 28.2 us  [call(): pl.pallas_call(kernel, out_shape=out_shape, in_specs=specs or [whole] * l...]
  transfers between devices with their start and end apart: 33 -> 36, of which waited for: 18 -> 16; matrix products, arithmetic and copies ran while one was open for 4% -> 4% of each run, Pallas kernels for 22% -> 23%
where the time goes in v2:
time: 106 us
  waiting for transfers between devices  39.2 us (37%)
  starting transfers between devices  32.6 us (31%)
  Pallas kernels  28.2 us (27%)
  other arithmetic  2.38 us (2%)
  local copies, waits for them, and re-layouts  2.37 us (2%)
  between operations  1.09 us (1%)
    ppermute x26, waiting for transfers between devices, permute_by(): return lax.ppermute(block, ('cfg', 'tok'), route)  36.5 us
    ppermute x26, starting transfers between devices, permute_by(): return lax.ppermute(block, ('cfg', 'tok'), route)  30.8 us
    pallas_call x13, Pallas kernels, call(): pl.pallas_call(kernel, out_shape=out_shape, in_specs=specs or [whole] * l...  28.2 us
    ppermute x10, waiting for transfers between devices, from_other_half(): return lax.ppermute(block, 'cfg', [(0, 1), (1, 0)])  2.65 us
  transfers between devices with their start and end apart: 36, of which 16 were waited for; matrix products, arithmetic and copies ran while one was open for 4% of the time, Pallas kernels for 23%

profile of v2, /device:TPU:0, one launch (start us, length us, event | category | flops | bytes accessed | tf_op | source)
XLA Modules:
  0.0 105.9 jit_solution(8849312478806677958)
XLA Ops:
  0.6 1.9 %first.1 = (bf16[64,1152]{1,0:T(8,128)(2,1)}, bf16[112,1152]{1,0:T(8,128)(2,1)}) custom-call(bf16[192,1152]{1,0:T(8,128)(2,1)} %hidden_ref.3, bf16[576,1152]{1,0:T(8,128)(2,1)} %bitcast.23, bf16[576,1152]{1,0:T(8,128)(2,1)} %bitcast.27), custom_call_target="tpu_custom_call" | custom-call | bytes 3096576 | tf_op jit(solution)/shard_map/first/pallas_call | solution.py:62
  2.5 3.0 %collective-permute-start = (bf16[64,1152]{1,0:T(8,128)(2,1)}, bf16[64,1152]{1,0:T(8,128)(2,1)S(1)}, u32[]{:S(2)}, u32[]{:S(2)}) collective-permute-start(bf16[64,1152]{1,0:T(8,128)(2,1)} %get-tuple-element.39), channel_id=1, source_target_pairs={{0,1},{1,0},{2,3},{3,2},{4,5},{5,4},{6,7},{7,6},{8,9},{9,8},{10,11... | collective-permute-start | bytes 442376 | tf_op jit(solution)/shard_map/ppermute | solution.py:33
  10.1 1.9 %collective-permute-start.1 = (bf16[200,1152]{1,0:T(8,128)(2,1)S(1)}, bf16[200,1152]{1,0:T(8,128)(2,1)S(1)}, u32[]{:S(2)}, u32[]{:S(2)}) collective-permute-start(bf16[200,1152]{1,0:T(8,128)(2,1)S(1)} %pad_maximum_fusion.1), channel_id=1, source_target_pairs={{0,2},{1,3},{2,0},{3,1},{4,6},{5,7},{6,4},{7,5},{8,10},{9,11},{10,... | collective-permute-start | bytes 1382408 | tf_op jit(solution)/shard_map/ppermute | solution.py:33
  12.1 2.6 %collective-permute-done.3.refs_3_.refs_0_ = bf16[112,1152]{1,0:T(8,128)(2,1)S(1)} collective-permute-done((bf16[112,1152]{1,0:T(8,128)(2,1)}, bf16[112,1152]{1,0:T(8,128)(2,1)S(1)}, u32[]{:S(2)}, u32[]{:S(2)}) %collective-permute-start.3) | collective-permute-done | bytes 258080 | tf_op jit(solution)/shard_map/ppermute | solution.py:33
  15.0 3.7 %collective-permute-done.1.refs_2_.refs_1_ = bf16[200,1152]{1,0:T(8,128)(2,1)S(1)} collective-permute-done((bf16[200,1152]{1,0:T(8,128)(2,1)S(1)}, bf16[200,1152]{1,0:T(8,128)(2,1)S(1)}, u32[]{:S(2)}, u32[]{:S(2)}) %collective-permute-start.1) | collective-permute-done | bytes 460832 | tf_op jit(solution)/shard_map/ppermute | solution.py:33
  18.8 2.0 %collective-permute-start.2 = (bf16[400,1152]{1,0:T(8,128)(2,1)S(1)}, bf16[400,1152]{1,0:T(8,128)(2,1)S(1)}, u32[]{:S(2)}, u32[]{:S(2)}) collective-permute-start(bf16[400,1152]{1,0:T(8,128)(2,1)S(1)} %get-tuple-element.77), channel_id=1, source_target_pairs={{0,4},{1,5},{2,6},{3,7},{4,0},{5,1},{6,2},{7,3},{8,12},{9,13},{10,... | collective-permute-start | bytes 2764808 | tf_op jit(solution)/shard_map/ppermute | solution.py:33
  25.1 2.5 %qkv_early.1 = (bf16[768,768]{1,0:T(8,128)(2,1)S(1)}, bf16[768,1152]{1,0:T(8,128)(2,1)S(1)}) custom-call(f32[2,8,1152]{2,1,0:T(8,128)S(1)} %bitcast.31, bf16[432,1152]{1,0:T(8,128)(2,1)S(1)} %bitcast.38, bf16[192,1152]{1,0:T(8,128)(2,1)S(1)} %copy-done.2, bf16[64,1152]{1,0:T(8,128)(2,1)S(1)} %collective-permute-done.refs_1_, ...), custom_call_target="tpu_custom_call" | custom-call | flops 1358954496 | bytes 3538944 | tf_op jit(solution)/shard_map/qkv_early/pallas_call | solution.py:62
  27.7 2.9 %collective-permute-done.5.refs_1_ = bf16[128,1152]{1,0:T(8,128)(2,1)S(1)} collective-permute-done((bf16[128,1152]{1,0:T(8,128)(2,1)S(1)}, bf16[128,1152]{1,0:T(8,128)(2,1)S(1)}, u32[]{:S(2)}, u32[]{:S(2)}) %collective-permute-start.5) | collective-permute-done | bytes 294944 | tf_op jit(solution)/shard_map/ppermute | solution.py:33
  30.6 1.7 %collective-permute-done.2.refs_0_.refs_2_ = bf16[400,1152]{1,0:T(8,128)(2,1)S(1)} collective-permute-done((bf16[400,1152]{1,0:T(8,128)(2,1)S(1)}, bf16[400,1152]{1,0:T(8,128)(2,1)S(1)}, u32[]{:S(2)}, u32[]{:S(2)}) %collective-permute-start.2) | collective-permute-done | bytes 921632 | tf_op jit(solution)/shard_map/ppermute | solution.py:33
  33.0 1.9 %collective-permute-start.13 = (bf16[288,1152]{1,0:T(8,128)(2,1)S(1)}, bf16[288,1152]{1,0:T(8,128)(2,1)S(1)}, u32[]{:S(2)}, u32[]{:S(2)}) collective-permute-start(bf16[288,1152]{1,0:T(8,128)(2,1)S(1)} %pad_maximum_fusion), channel_id=1, source_target_pairs={{0,1},{1,0},{2,3},{3,2},{4,5},{5,4},{6,7},{7,6},{8,9},{9,8},{10,11... | collective-permute-start | bytes 1990664 | tf_op jit(solution)/shard_map/ppermute | solution.py:33
  36.4 1.6 %qkv_late_own.1.refs_0_ = bf16[384,768]{1,0:T(8,128)(2,1)S(1)} custom-call(f32[2,8,1152]{2,1,0:T(8,128)S(1)} %bitcast.32, bf16[768,1152]{1,0:T(8,128)(2,1)S(1)} %get-tuple-element.47.weight_ref, bf16[400,1152]{1,0:T(8,128)(2,1)S(1)} %collective-permute-done.2.refs_0_.refs_2_, bf16[128,1152]{1,0:T(8,128)(2,1)S(1)} %collective-permute-done.5.refs_1_), custom_call_target="tpu_custom_call" | custom-call | flops 679477248 | bytes 3059712 | tf_op jit(solution)/shard_map/qkv_late_own/pallas_call | solution.py:62
  38.1 1.6 %qkv_late_other.1.refs_1_ = bf16[384,768]{1,0:T(8,128)(2,1)S(1)} custom-call(f32[2,8,1152]{2,1,0:T(8,128)S(1)} %bitcast.33, bf16[768,1152]{1,0:T(8,128)(2,1)S(1)} %get-tuple-element.47.weight_ref, bf16[400,1152]{1,0:T(8,128)(2,1)S(1)} %collective-permute-done.10.refs_0_.refs_6_, bf16[128,1152]{1,0:T(8,128)(2,1)S(1)} %collective-permute-done.11.refs_1_), custom_call_target="tpu_custom_call" | custom-call | flops 679477248 | bytes 3059712 | tf_op jit(solution)/shard_map/qkv_late_other/pallas_call | solution.py:62
  39.7 6.2 %attend.1 = (bf16[144,768]{1,0:T(8,128)(2,1)S(1)}, bf16[144,768]{1,0:T(8,128)(2,1)S(1)}) custom-call(s32[2,8]{1,0:T(2,128)S(1)} %copy-done.6, bf16[768,768]{1,0:T(8,128)(2,1)S(1)} %get-tuple-element.44.early_ref, bf16[384,768]{1,0:T(8,128)(2,1)S(1)} %qkv_late_own.1.refs_0_, bf16[384,768]{1,0:T(8,128)(2,1)S(1)} %qkv_late_other.1.refs_1_), custom_call_target="tpu_custom_call" | custom-call | flops 1358954496 | bytes 2359360 | tf_op jit(solution)/shard_map/attend/pallas_call | solution.py:62
  46.7 5.3 %collective-permute-done.12.mate_ref = bf16[144,768]{1,0:T(8,128)(2,1)S(1)} collective-permute-done((bf16[144,768]{1,0:T(8,128)(2,1)S(1)}, bf16[144,768]{1,0:T(8,128)(2,1)S(1)}, u32[]{:S(2)}, u32[]{:S(2)}) %collective-permute-start.12) | collective-permute-done | bytes 221216 | tf_op jit(solution)/shard_map/ppermute | solution.py:33
  54.4 1.6 %collective-permute-start.18 = (bf16[144,384]{1,0:T(8,128)(2,1)S(1)}, bf16[144,384]{1,0:T(8,128)(2,1)S(1)}, u32[]{:S(2)}, u32[]{:S(2)}) collective-permute-start(bf16[144,384]{1,0:T(8,128)(2,1)S(1)} %pad_maximum_fusion.10), channel_id=1, source_target_pairs={{0,6},{1,7},{2,4},{3,5},{4,2},{5,3},{6,0},{7,1},{8,14},{9,15},{10,... | collective-permute-start | bytes 331784 | tf_op jit(solution)/shard_map/ppermute | solution.py:33
  57.0 2.4 %collective-permute-done.17.refs_9_ = bf16[144,384]{1,0:T(8,128)(2,1)S(1)} collective-permute-done((bf16[144,384]{1,0:T(8,128)(2,1)S(1)}, bf16[144,384]{1,0:T(8,128)(2,1)S(1)}, u32[]{:S(2)}, u32[]{:S(2)}) %collective-permute-start.17) | collective-permute-done | bytes 110624 | tf_op jit(solution)/shard_map/ppermute | solution.py:33
  59.4 1.7 %collective-permute-done.18.refs_10_ = bf16[144,384]{1,0:T(8,128)(2,1)S(1)} collective-permute-done((bf16[144,384]{1,0:T(8,128)(2,1)S(1)}, bf16[144,384]{1,0:T(8,128)(2,1)S(1)}, u32[]{:S(2)}, u32[]{:S(2)}) %collective-permute-start.18) | collective-permute-done | bytes 110624 | tf_op jit(solution)/shard_map/ppermute | solution.py:33
  61.9 1.9 %project.1 = (f32[192,1152]{1,0:T(8,128)S(1)}, bf16[192,1152]{1,0:T(8,128)(2,1)S(1)}) custom-call(f32[2,8,1152]{2,1,0:T(8,128)S(1)} %bitcast.34, bf16[192,1152]{1,0:T(8,128)(2,1)S(1)} %copy-done.2, bf16[144,768]{1,0:T(8,128)(2,1)S(1)} %get-tuple-element.51.mine_ref, bf16[144,768]{1,0:T(8,128)(2,1)S(1)} %collective-permute-done.12.mate_ref, ...), custom_call_target="tpu_custom_call" | custom-call | flops 509607936 | bytes 5713920 | tf_op jit(solution)/shard_map/project/pallas_call | solution.py:62
  64.5 7.7 %collective-permute-done.20.refs_1_ = bf16[192,1152]{1,0:T(8,128)(2,1)S(1)} collective-permute-done((bf16[192,1152]{1,0:T(8,128)(2,1)S(1)}, bf16[192,1152]{1,0:T(8,128)(2,1)S(1)}, u32[]{:S(2)}, u32[]{:S(2)}) %collective-permute-start.20) | collective-permute-done | bytes 442400 | tf_op jit(solution)/shard_map/ppermute | solution.py:33
  76.6 2.0 %pack.1 = (bf16[1152,1152]{1,0:T(8,128)(2,1)S(1)}, bf16[1152,1152]{1,0:T(8,128)(2,1)S(1)}) custom-call(bf16[576,1152]{1,0:T(8,128)(2,1)S(1)} %bitcast.26, bf16[576,1152]{1,0:T(8,128)(2,1)S(1)} %bitcast.30, bf16[112,1152]{1,0:T(8,128)(2,1)S(1)} %collective-permute-done.3.refs_3_.refs_0_, bf16[320,1152]{1,0:T(8,128)(2,1)S(1)} %collective-permute-done.15.refs_1_, ...), custom_call_target="tpu_custom_call" | custom-call | bytes 5455872 | tf_op jit(solution)/shard_map/pack/pallas_call | solution.py:62
  88.8 2.7 %mlp_near.1 = (f32[192,1152]{1,0:T(8,128)S(1)}, f32[48,1152]{1,0:T(8,128)S(1)}, f32[48,1152]{1,0:T(8,128)S(1)}, f32[48,1152]{1,0:T(8,128)S(1)}, f32[48,1152]{1,0:T(8,128)S(1)}) custom-call(bf16[1152,1152]{1,0:T(8,128)(2,1)S(1)} %get-tuple-element.65.up_ref, bf16[1152,1152]{1,0:T(8,128)(2,1)S(1)} %get-tuple-element.66.down_ref, ...), custom_call_target="tpu_custom_call" | custom-call | flops 2038431744 | bytes 6193152 | tf_op jit(solution)/shard_map/mlp_near/pallas_call | solution.py:62
  94.4 2.9 %collective-permute-done.30.refs_3_ = bf16[96,1152]{1,0:T(8,128)(2,1)S(1)} collective-permute-done((bf16[96,1152]{1,0:T(8,128)(2,1)S(1)}, bf16[96,1152]{1,0:T(8,128)(2,1)S(1)}, u32[]{:S(2)}, u32[]{:S(2)}) %collective-permute-start.30) | collective-permute-done | bytes 221216 | tf_op jit(solution)/shard_map/ppermute | solution.py:33
  98.8 3.3 %collective-permute-done.34.refs_7_ = bf16[48,1152]{1,0:T(8,128)(2,1)S(1)} collective-permute-done((bf16[48,1152]{1,0:T(8,128)(2,1)S(1)}, bf16[48,1152]{1,0:T(8,128)(2,1)S(1)}, u32[]{:S(2)}, u32[]{:S(2)}) %collective-permute-start.34) | collective-permute-done | bytes 110624 | tf_op jit(solution)/shard_map/ppermute | solution.py:33
  102.1 1.9 %finish.1 = (bf16[192,1152]{1,0:T(8,128)(2,1)}, f32[16,192]{1,0:T(8,128)S(1)}, f32[16,192]{1,0:T(8,128)S(1)}) custom-call(s32[2,8]{1,0:T(2,128)S(1)} %copy-done.6, f32[2]{0:T(128)S(1)} %copy-done.8, f32[2,2]{1,0:T(2,128)S(1)} %copy-done.7, f32[2,8,1152]{2,1,0:T(8,128)S(1)} %bitcast.35, f32[192,1152]{1,0:T(8,128)S(1)} %get-tuple-element.59.mid_ref, ...), custom_call_target="tpu_custom_call" | custom-call | flops 7077888 | bytes 3219544 | tf_op jit(solution)/shard_map/finish/pallas_call | solution.py:62
  (114 shorter events, 37.7 us)
Async XLA Ops:
  2.5 6.5 %collective-permute-start = (bf16[64,1152]{1,0:T(8,128)(2,1)}, bf16[64,1152]{1,0:T(8,128)(2,1)S(1)}, u32[]{:S(2)}, u32[]{:S(2)}) collective-permute-start(bf16[64,1152]{1,0:T(8,128)(2,1)} %get-tuple-element.39), channel_id=1, source_target_pairs={{0,1},{1,0},{2,3},{3,2},{4,5},{5,4},{6,7},{7,6},{8,9},{9,8},{10,11... | collective-permute-start | bytes 442376 | tf_op jit(solution)/shard_map/ppermute | solution.py:33
  5.5 9.2 %collective-permute-start.3 = (bf16[112,1152]{1,0:T(8,128)(2,1)}, bf16[112,1152]{1,0:T(8,128)(2,1)S(1)}, u32[]{:S(2)}, u32[]{:S(2)}) collective-permute-start(bf16[112,1152]{1,0:T(8,128)(2,1)} %get-tuple-element.40), channel_id=1, source_target_pairs={{0,4},{1,5},{2,6},{3,7},{4,0},{5,1},{6,2},{7,3},{8,12},{9,13},{10,... | collective-permute-start | bytes 774152 | tf_op jit(solution)/shard_map/ppermute | solution.py:33
  10.1 8.6 %collective-permute-start.1 = (bf16[200,1152]{1,0:T(8,128)(2,1)S(1)}, bf16[200,1152]{1,0:T(8,128)(2,1)S(1)}, u32[]{:S(2)}, u32[]{:S(2)}) collective-permute-start(bf16[200,1152]{1,0:T(8,128)(2,1)S(1)} %pad_maximum_fusion.1), channel_id=1, source_target_pairs={{0,2},{1,3},{2,0},{3,1},{4,6},{5,7},{6,4},{7,5},{8,10},{9,11},{10,... | collective-permute-start | bytes 1382408 | tf_op jit(solution)/shard_map/ppermute | solution.py:33
  14.7 6.8 %collective-permute-start.4 = (bf16[64,1152]{1,0:T(8,128)(2,1)S(1)}, bf16[64,1152]{1,0:T(8,128)(2,1)S(1)}, u32[]{:S(2)}, u32[]{:S(2)}) collective-permute-start(bf16[64,1152]{1,0:T(8,128)(2,1)S(1)} %pad_maximum_fusion.7), channel_id=1, source_target_pairs={{0,1},{1,0},{2,3},{3,2},{4,5},{5,4},{6,7},{7,6},{8,9},{9,8},{10,11... | collective-permute-start | bytes 442376 | tf_op jit(solution)/shard_map/ppermute | solution.py:33
  18.8 13.5 %collective-permute-start.2 = (bf16[400,1152]{1,0:T(8,128)(2,1)S(1)}, bf16[400,1152]{1,0:T(8,128)(2,1)S(1)}, u32[]{:S(2)}, u32[]{:S(2)}) collective-permute-start(bf16[400,1152]{1,0:T(8,128)(2,1)S(1)} %get-tuple-element.77), channel_id=1, source_target_pairs={{0,4},{1,5},{2,6},{3,7},{4,0},{5,1},{6,2},{7,3},{8,12},{9,13},{10,... | collective-permute-start | bytes 2764808 | tf_op jit(solution)/shard_map/ppermute | solution.py:33
  21.5 9.1 %collective-permute-start.5 = (bf16[128,1152]{1,0:T(8,128)(2,1)S(1)}, bf16[128,1152]{1,0:T(8,128)(2,1)S(1)}, u32[]{:S(2)}, u32[]{:S(2)}) collective-permute-start(bf16[128,1152]{1,0:T(8,128)(2,1)S(1)} %pad_maximum_fusion.2), channel_id=1, source_target_pairs={{0,2},{1,3},{2,0},{3,1},{4,6},{5,7},{6,4},{7,5},{8,10},{9,11},{10,... | collective-permute-start | bytes 884744 | tf_op jit(solution)/shard_map/ppermute | solution.py:33
  32.3 5.8 %collective-permute-start.10 = (bf16[400,1152]{1,0:T(8,128)(2,1)S(1)}, bf16[400,1152]{1,0:T(8,128)(2,1)S(1)}, u32[]{:S(2)}, u32[]{:S(2)}) collective-permute-start(bf16[400,1152]{1,0:T(8,128)(2,1)S(1)} %collective-permute-done.2.refs_0_.refs_2_), channel_id=1, source_target_pairs={{0,16},{16,0},{1,17},{17,1},{2,18},{18,2},{3,19},{19,3},{4,20},{20... | collective-permute-start | bytes 2764808 | tf_op jit(solution)/shard_map/ppermute | solution.py:37
  33.0 13.7 %collective-permute-start.13 = (bf16[288,1152]{1,0:T(8,128)(2,1)S(1)}, bf16[288,1152]{1,0:T(8,128)(2,1)S(1)}, u32[]{:S(2)}, u32[]{:S(2)}) collective-permute-start(bf16[288,1152]{1,0:T(8,128)(2,1)S(1)} %pad_maximum_fusion), channel_id=1, source_target_pairs={{0,1},{1,0},{2,3},{3,2},{4,5},{5,4},{6,7},{7,6},{8,9},{9,8},{10,11... | collective-permute-start | bytes 1990664 | tf_op jit(solution)/shard_map/ppermute | solution.py:33
  34.9 21.2 %collective-permute-start.15 = (bf16[320,1152]{1,0:T(8,128)(2,1)S(1)}, bf16[320,1152]{1,0:T(8,128)(2,1)S(1)}, u32[]{:S(2)}, u32[]{:S(2)}) collective-permute-start(bf16[320,1152]{1,0:T(8,128)(2,1)S(1)} %slice_select_fusion), channel_id=1, source_target_pairs={{0,4},{1,5},{2,6},{3,7},{4,0},{5,1},{6,2},{7,3},{8,12},{9,13},{10,... | collective-permute-start | bytes 2211848 | tf_op jit(solution)/shard_map/ppermute | solution.py:33
  45.9 6.0 %collective-permute-start.12 = (bf16[144,768]{1,0:T(8,128)(2,1)S(1)}, bf16[144,768]{1,0:T(8,128)(2,1)S(1)}, u32[]{:S(2)}, u32[]{:S(2)}) collective-permute-start(bf16[144,768]{1,0:T(8,128)(2,1)S(1)} %get-tuple-element.52), channel_id=1, source_target_pairs={{0,1},{1,0},{2,3},{3,2},{4,5},{5,4},{6,7},{7,6},{8,9},{9,8},{10,11... | collective-permute-start | bytes 663560 | tf_op jit(solution)/shard_map/ppermute | solution.py:33
  51.9 10.0 %collective-permute-start.14 = (bf16[288,1152]{1,0:T(8,128)(2,1)S(1)}, bf16[288,1152]{1,0:T(8,128)(2,1)S(1)}, u32[]{:S(2)}, u32[]{:S(2)}) collective-permute-start(bf16[288,1152]{1,0:T(8,128)(2,1)S(1)} %collective-permute-done.13.refs_3_), channel_id=1, source_target_pairs={{0,16},{16,0},{1,17},{17,1},{2,18},{18,2},{3,19},{19,3},{4,20},{20... | collective-permute-start | bytes 1990664 | tf_op jit(solution)/shard_map/ppermute | solution.py:37
  54.4 6.6 %collective-permute-start.18 = (bf16[144,384]{1,0:T(8,128)(2,1)S(1)}, bf16[144,384]{1,0:T(8,128)(2,1)S(1)}, u32[]{:S(2)}, u32[]{:S(2)}) collective-permute-start(bf16[144,384]{1,0:T(8,128)(2,1)S(1)} %pad_maximum_fusion.10), channel_id=1, source_target_pairs={{0,6},{1,7},{2,4},{3,5},{4,2},{5,3},{6,0},{7,1},{8,14},{9,15},{10,... | collective-permute-start | bytes 331784 | tf_op jit(solution)/shard_map/ppermute | solution.py:33
  61.0 11.3 %collective-permute-start.19 = (bf16[176,1152]{1,0:T(8,128)(2,1)S(1)}, bf16[176,1152]{1,0:T(8,128)(2,1)S(1)}, u32[]{:S(2)}, u32[]{:S(2)}) collective-permute-start(bf16[176,1152]{1,0:T(8,128)(2,1)S(1)} %slice_select_fusion.1), channel_id=1, source_target_pairs={{0,4},{1,5},{2,6},{3,7},{4,0},{5,1},{6,2},{7,3},{8,12},{9,13},{10,... | collective-permute-start | bytes 1216520 | tf_op jit(solution)/shard_map/ppermute | solution.py:33
  61.9 13.7 %collective-permute-start.21 = (bf16[320,1152]{1,0:T(8,128)(2,1)S(1)}, bf16[320,1152]{1,0:T(8,128)(2,1)S(1)}, u32[]{:S(2)}, u32[]{:S(2)}) collective-permute-start(bf16[320,1152]{1,0:T(8,128)(2,1)S(1)} %collective-permute-done.15.refs_1_), channel_id=1, source_target_pairs={{0,16},{16,0},{1,17},{17,1},{2,18},{18,2},{3,19},{19,3},{4,20},{20... | collective-permute-start | bytes 2211848 | tf_op jit(solution)/shard_map/ppermute | solution.py:37
  63.8 8.4 %collective-permute-start.20 = (bf16[192,1152]{1,0:T(8,128)(2,1)S(1)}, bf16[192,1152]{1,0:T(8,128)(2,1)S(1)}, u32[]{:S(2)}, u32[]{:S(2)}) collective-permute-start(bf16[192,1152]{1,0:T(8,128)(2,1)S(1)} %get-tuple-element.67.refs_0_), channel_id=1, source_target_pairs={{0,1},{1,0},{2,3},{3,2},{4,5},{5,4},{6,7},{7,6},{8,9},{9,8},{10,11... | collective-permute-start | bytes 1327112 | tf_op jit(solution)/shard_map/ppermute | solution.py:33
  72.4 6.2 %collective-permute-start.23 = (bf16[96,1152]{1,0:T(8,128)(2,1)S(1)}, bf16[96,1152]{1,0:T(8,128)(2,1)S(1)}, u32[]{:S(2)}, u32[]{:S(2)}) collective-permute-start(bf16[96,1152]{1,0:T(8,128)(2,1)S(1)} %pad_maximum_fusion.3), channel_id=1, source_target_pairs={{0,2},{1,3},{2,0},{3,1},{4,6},{5,7},{6,4},{7,5},{8,10},{9,11},{10,... | collective-permute-start | bytes 663560 | tf_op jit(solution)/shard_map/ppermute | solution.py:33
  73.5 7.6 %collective-permute-start.24 = (bf16[96,1152]{1,0:T(8,128)(2,1)S(1)}, bf16[96,1152]{1,0:T(8,128)(2,1)S(1)}, u32[]{:S(2)}, u32[]{:S(2)}) collective-permute-start(bf16[96,1152]{1,0:T(8,128)(2,1)S(1)} %pad_maximum_fusion.4), channel_id=1, source_target_pairs={{0,2},{1,3},{2,0},{3,1},{4,6},{5,7},{6,4},{7,5},{8,10},{9,11},{10,... | collective-permute-start | bytes 663560 | tf_op jit(solution)/shard_map/ppermute | solution.py:33
  74.5 9.2 %collective-permute-start.25 = (bf16[96,1152]{1,0:T(8,128)(2,1)S(1)}, bf16[96,1152]{1,0:T(8,128)(2,1)S(1)}, u32[]{:S(2)}, u32[]{:S(2)}) collective-permute-start(bf16[96,1152]{1,0:T(8,128)(2,1)S(1)} %pad_maximum_fusion.5), channel_id=1, source_target_pairs={{0,2},{1,3},{2,0},{3,1},{4,6},{5,7},{6,4},{7,5},{8,10},{9,11},{10,... | collective-permute-start | bytes 663560 | tf_op jit(solution)/shard_map/ppermute | solution.py:33
  75.6 10.7 %collective-permute-start.26 = (bf16[96,1152]{1,0:T(8,128)(2,1)S(1)}, bf16[96,1152]{1,0:T(8,128)(2,1)S(1)}, u32[]{:S(2)}, u32[]{:S(2)}) collective-permute-start(bf16[96,1152]{1,0:T(8,128)(2,1)S(1)} %pad_maximum_fusion.6), channel_id=1, source_target_pairs={{0,2},{1,3},{2,0},{3,1},{4,6},{5,7},{6,4},{7,5},{8,10},{9,11},{10,... | collective-permute-start | bytes 663560 | tf_op jit(solution)/shard_map/ppermute | solution.py:33
  80.1 11.5 %collective-permute-start.27 = (bf16[96,1152]{1,0:T(8,128)(2,1)S(1)}, bf16[96,1152]{1,0:T(8,128)(2,1)S(1)}, u32[]{:S(2)}, u32[]{:S(2)}) collective-permute-start(bf16[96,1152]{1,0:T(8,128)(2,1)S(1)} %mlp_far0.1), channel_id=1, source_target_pairs={{0,2},{1,3},{2,0},{3,1},{4,6},{5,7},{6,4},{7,5},{8,10},{9,11},{10,... | collective-permute-start | bytes 663560 | tf_op jit(solution)/shard_map/ppermute | solution.py:33
  82.6 9.5 %collective-permute-start.28 = (bf16[96,1152]{1,0:T(8,128)(2,1)S(1)}, bf16[96,1152]{1,0:T(8,128)(2,1)S(1)}, u32[]{:S(2)}, u32[]{:S(2)}) collective-permute-start(bf16[96,1152]{1,0:T(8,128)(2,1)S(1)} %mlp_far1.1), channel_id=1, source_target_pairs={{0,2},{1,3},{2,0},{3,1},{4,6},{5,7},{6,4},{7,5},{8,10},{9,11},{10,... | collective-permute-start | bytes 663560 | tf_op jit(solution)/shard_map/ppermute | solution.py:33
  85.1 8.6 %collective-permute-start.29 = (bf16[96,1152]{1,0:T(8,128)(2,1)S(1)}, bf16[96,1152]{1,0:T(8,128)(2,1)S(1)}, u32[]{:S(2)}, u32[]{:S(2)}) collective-permute-start(bf16[96,1152]{1,0:T(8,128)(2,1)S(1)} %mlp_far2.1), channel_id=1, source_target_pairs={{0,2},{1,3},{2,0},{3,1},{4,6},{5,7},{6,4},{7,5},{8,10},{9,11},{10,... | collective-permute-start | bytes 663560 | tf_op jit(solution)/shard_map/ppermute | solution.py:33
  87.7 9.6 %collective-permute-start.30 = (bf16[96,1152]{1,0:T(8,128)(2,1)S(1)}, bf16[96,1152]{1,0:T(8,128)(2,1)S(1)}, u32[]{:S(2)}, u32[]{:S(2)}) collective-permute-start(bf16[96,1152]{1,0:T(8,128)(2,1)S(1)} %mlp_far3.1), channel_id=1, source_target_pairs={{0,2},{1,3},{2,0},{3,1},{4,6},{5,7},{6,4},{7,5},{8,10},{9,11},{10,... | collective-permute-start | bytes 663560 | tf_op jit(solution)/shard_map/ppermute | solution.py:33
  91.6 5.8 %collective-permute-start.31 = (bf16[48,1152]{1,0:T(8,128)(2,1)S(1)}, bf16[48,1152]{1,0:T(8,128)(2,1)S(1)}, u32[]{:S(2)}, u32[]{:S(2)}) collective-permute-start(bf16[48,1152]{1,0:T(8,128)(2,1)S(1)} %add_convert_fusion.3), channel_id=1, source_target_pairs={{0,1},{1,0},{2,3},{3,2},{4,5},{5,4},{6,7},{7,6},{8,9},{9,8},{10,11... | collective-permute-start | bytes 331784 | tf_op jit(solution)/shard_map/ppermute | solution.py:33
  (23 other events, 132.6 us)
